TPU v7x, 128 devices: a whole 4x4x4 slice. The times are simulated.
128 devices in a mesh: dp: 2 (over core), row: 8 (over y, x_lo), col: 8 (over x_hi, z).
Axes of the slice: x: 4 (x_hi: 2, x_lo: 2; x = x_hi * 2 + x_lo), y: 4, z: 4, core: 2. Of those that a mesh axis runs over, the one named last changes fastest.
Arguments:
- tokens: bfloat16 [8192, 6144], P(('dp', 'row'), 'col'), may hold values from -6 to 6
- w_qkv: bfloat16 [6144, 9216], P(('dp', 'row'), 'col'), may hold values from -0.078125 to 0.078125
- w_out: bfloat16 [3072, 6144], P(('dp', 'row'), 'col'), may hold values from -0.109375 to 0.109375
- ada_shift: float32 [2, 6144], P('dp'), may hold values from -3 to 3
- ada_scale: float32 [2, 6144], P('dp'), may hold values from -3 to 3
- out_gate: float32 [2, 6144], P('dp', 'col'), may hold values from 0.5 to 2
- head_gain: float32 [24], P('col'), may hold values from 1 to 4
- block_segment: int32 [2, 32], P('dp'), may hold values from 0 to 7, never falling along the last dimension, each value on 1 to 16 neighbouring positions
Outputs:
- mixed: bfloat16 [8192, 6144], P(('dp', 'row'), 'col')
Inputs may be any that keep to these rules, and one draw needn't show every extreme that they name: `block_segment`: in each replica's row the numbers never fall; each request covers 1 to 16 consecutive blocks, and one covers exactly 16.
All inputs are finite; a program needn't handle non-finite values.
Results may differ from a plain program's by a relative error of at most 0.01.
Values may be sent and summed in bfloat16 or wider, within the bound.
A program may use at most 128 MiB of HBM per device.

v0:
```python
import jax
import jax.numpy as jnp
from jax import lax
from jax.sharding import PartitionSpec as P

HD = 128
BLK = 128


def rms_norm(vector):
    return vector * lax.rsqrt(jnp.mean(vector * vector, axis=-1, keepdims=True) + 1e-06)


def joint_fold(left, piece):
    return jnp.dot(left, piece, preferred_element_type=jnp.float32)


def local(tokens, w_qkv, w_out, ada_shift, ada_scale, out_gate, head_gain, block_segment):
    tok_rows = tokens.shape[0]
    heads_here = head_gain.shape[0]
    inverse = 1.0 / HD**0.5
    x_panel = lax.all_gather(tokens, "col", axis=1, tiled=True)
    x_float = x_panel.astype(jnp.float32)
    row_mean = jnp.mean(x_float, axis=-1, keepdims=True)
    centred = x_float - row_mean
    variance = jnp.mean(centred * centred, axis=-1, keepdims=True)
    normed = centred * lax.rsqrt(variance + 1e-06)
    modulated = (normed * (1.0 + ada_scale[0]) + ada_shift[0]).astype(jnp.bfloat16)
    projected = joint_fold(modulated, lax.all_gather(w_qkv, ("dp", "row"), axis=0, tiled=True))
    projected = projected.reshape(tok_rows, heads_here, 3, HD)
    query = (rms_norm(projected[:, :, 0]) * head_gain[None, :, None]).astype(jnp.bfloat16)
    keys_local = (
        rms_norm(projected[:, :, 1]).astype(jnp.bfloat16).reshape(tok_rows, heads_here * HD)
    )
    values_local = projected[:, :, 2].astype(jnp.bfloat16).reshape(tok_rows, heads_here * HD)
    token_segment = jnp.repeat(block_segment[0], BLK)
    query_segment = lax.dynamic_slice_in_dim(
        token_segment, lax.axis_index("row") * tok_rows, tok_rows
    )
    start_state = (
        jnp.zeros((tok_rows, heads_here, HD), jnp.float32),
        jnp.zeros((heads_here, tok_rows), jnp.float32),
    )
    pieces = (
        lax.all_gather(keys_local, "row", axis=0, tiled=True),
        lax.all_gather(values_local, "row", axis=0, tiled=True),
    )
    key_piece = pieces[0].reshape(pieces[0].shape[0], heads_here, HD)
    value_piece = pieces[1].reshape(pieces[1].shape[0], heads_here, HD)
    same_mask = (query_segment[:, None] == token_segment[None, :]).astype(jnp.float32)

    def compute(state):
        scores = (
            jnp.einsum("thd,shd->hts", query, key_piece, preferred_element_type=jnp.float32)
            * inverse
        )
        weights = jnp.exp(scores) * same_mask[None]
        rounded = weights.astype(jnp.bfloat16)
        numer = jnp.einsum("hts,shd->thd", rounded, value_piece, preferred_element_type=jnp.float32)
        return (numer, jnp.sum(weights, axis=-1))

    def unchanged(state):
        return state

    numer, totals = lax.cond(jnp.any(same_mask > 0.0), compute, unchanged, start_state)
    attended = (
        (numer / jnp.transpose(totals)[:, :, None])
        .astype(jnp.bfloat16)
        .reshape(tok_rows, heads_here * HD)
    )
    heads_all = lax.all_gather(attended, "col", axis=1, tiled=True)
    branch = joint_fold(heads_all, lax.all_gather(w_out, ("dp", "row"), axis=0, tiled=True))
    return (out_gate[0] * branch).astype(jnp.bfloat16)


def solution(mesh):
    placed = (
        P(("dp", "row"), "col"),
        P(("dp", "row"), "col"),
        P(("dp", "row"), "col"),
        P("dp", None),
        P("dp", None),
        P("dp", "col"),
        P("col"),
        P("dp", None),
    )
    return jax.shard_map(
        local, mesh=mesh, in_specs=placed, out_specs=P(("dp", "row"), "col"), check_vma=False
    )
```

profile of v0, /device:TPU:1, one launch (start us, length us, event | category | flops | bytes accessed | tf_op | source)
XLA Modules:
  0.0 459.2 jit_solution(1440865339292644298)
XLA Ops:
  6.5 0.0 copy-start
  6.5 0.0 copy-start.6
  6.5 0.0 all-gather.7.cloned.1.call-start
  6.5 0.7 all-gather.7.cloned.1.call-update
  7.3 0.0 all-gather.9.cloned.1.call-start
  7.3 0.7 all-gather.9.cloned.1.call-update
  8.0 0.0 all-gather.11.cloned.1.call-start
  8.1 0.8 broadcast_add_fusion
  8.8 92.3 %all-gather.7.cloned.1.call-done = bf16[512,6144]{1,0:T(8,128)(2,1)} async-done(((bf16[512,768]{1,0:T(8,128)(2,1)}), bf16[512,6144]{1,0:T(8,128)(2,1)}) %all-gather.7.cloned.1.call-update) | async-done | bytes 6291472 | tf_op jit(solution)/shard_map/all_gather | solution.py:22
  101.1 0.0 copy-start.2
  101.1 3.8 convert_reduce_fusion
  104.9 0.7 copy-done.2
  105.7 1.8 fusion.10
  107.5 73.2 %all-gather.9.cloned.1.call-done = bf16[6144,1152]{1,0:T(8,128)(2,1)} async-done(((bf16[384,1152]{1,0:T(8,128)(2,1)}), bf16[6144,1152]{1,0:T(8,128)(2,1)}) %all-gather.9.cloned.1.call-update) | async-done | bytes 14155792 | tf_op jit(solution)/shard_map/all_gather | solution.py:29
  180.7 0.0 copy-done.6
  180.7 14.8 %fusion.14 = f32[512,1152]{0,1:T(8,128)S(1)} fusion(bf16[6144,1152]{1,0:T(8,128)(2,1)} %all-gather.9.cloned.1.call-done, bf16[512,6144]{1,0:T(8,128)(2,1)} %all-gather.7.cloned.1.call-done, f32[6144]{0:T(1024)S(1)} %bitcast.42, f32[6144]{0:T(1024)S(1)} %bitcast.41, f32[512]{0:T(512)S(1)} %add_rsqrt_fusion.2, f32[512]{0:T(512)S(1)} %broadcast_multiply_fusion), kind=kOutput, calls=%fused_computation.16 | convolution fusion | flops 7266631680 | bytes 22859776 | tf_op jit(solution)/shard_map/dot_general | solution.py:15
  195.4 0.0 copy-start.5
  195.5 0.1 multiply_reduce_fusion.1
  195.6 0.8 fusion.20
  196.4 0.0 all-gather.11.cloned.1.call-update
  196.4 0.0 all-gather.13.cloned.1.call-start
  196.5 0.8 slice.23
  197.3 0.0 all-gather.13.cloned.1.call-update
  197.3 0.0 all-gather.17.cloned.1.call-start
  197.3 0.5 all-gather.17.cloned.1.call-update
  197.9 0.0 all-gather.15.cloned.1.call-start
  197.9 0.0 copy-done
  197.9 0.1 broadcast_bitcast_fusion
  198.0 0.1 dynamic_slice.3
  198.1 5.2 %compare_convert_fusion = (f32[512,4096]{1,0:T(8,128)}, pred[]{:T(512)}) fusion(s32[4096]{0:T(1024)S(1)} %broadcast_bitcast_fusion, s32[512]{0:T(512)S(1)} %dynamic_slice.3), kind=kLoop, calls=%fused_computation.15 | loop fusion | flops 8388607 | bytes 8407041 | tf_op jit(solution)/shard_map/convert_element_type | solution.py:50
  203.8 0.1 multiply_reduce_fusion
  203.9 0.0 copy-done.5
  203.9 0.1 multiply_convert_fusion.1
  204.1 64.3 %all-gather.11.cloned.1.call-done = bf16[4096,384]{0,1:T(8,128)(2,1)} async-done(((bf16[512,384]{0,1:T(8,128)(2,1)}), bf16[4096,384]{0,1:T(8,128)(2,1)}) %all-gather.11.cloned.1.call-update) | async-done | bytes 3145744 | tf_op jit(solution)/shard_map/all_gather | solution.py:45
  268.3 72.6 %all-gather.13.cloned.1.call-done = bf16[4096,384]{0,1:T(8,128)(2,1)} async-done(((bf16[512,384]{0,1:T(8,128)(2,1)}), bf16[4096,384]{0,1:T(8,128)(2,1)}) %all-gather.13.cloned.1.call-update) | async-done | bytes 3145744 | tf_op jit(solution)/shard_map/all_gather | solution.py:46
  340.9 31.5 %conditional.1 = (f32[3,512]{1,0:T(4,128)S(1)}, f32[512,3,128]{0,2,1:T(8,128)}) conditional(s32[]{:T(128)} %convert_element_type.34, () %tuple.13, (bf16[4096,384]{0,1:T(8,128)(2,1)}, bf16[512,3,128]{0,2,1:T(8,128)(2,1)S(1)}, f32[512,4096]{1,0:T(8,128)}, bf16[4096,384]{0,1:T(8,128)(2,1)}) %tuple.14), branch_computations={%region_5.0_spmd, %region_6.0_spmd} | conditional | flops 3258972672 | bytes 88741936 | solution.py:65
  340.9 15.0 %fusion = (f32[3,512]{1,0:T(4,128)S(1)}, f32[3,512,4096]{2,1,0:T(8,128)}) fusion(f32[512,4096]{1,0:T(8,128)} %get-tuple-element.17, bf16[512,3,128]{0,2,1:T(8,128)(2,1)S(1)} %get-tuple-element.24, bf16[4096,3,128]{0,2,1:T(8,128)(2,1)} %bitcast.36), kind=kOutput, calls=%fused_computation.1 | convolution fusion | flops 1629485568 | bytes 37099520 | tf_op jit(solution)/shard_map/cond/branch_1_fun/thd,shd->hts/dot_general | solution.py:54
  355.9 0.0 copy-done.3
  355.9 14.2 %fusion.4 = f32[512,3,128]{2,0,1:T(8,128)} fusion(bf16[4096,3,128]{0,2,1:T(8,128)(2,1)S(1)} %bitcast.37, f32[3,512,4096]{2,1,0:T(8,128)} %get-tuple-element.29, f32[512,4096]{1,0:T(8,128)} %get-tuple-element.17), kind=kOutput, calls=%fused_computation.4 | convolution fusion | flops 1629487104 | bytes 37486592 | tf_op jit(solution)/shard_map/cond/branch_1_fun/hts,shd->thd/dot_general | solution.py:59
  370.1 2.3 copy.23
  372.4 2.0 divide_convert_fusion
  374.3 0.0 all-gather.15.cloned.1.call-update
  374.4 0.0 copy-done.4
  374.4 0.0 copy-start.1
  374.4 6.6 %all-gather.17.cloned.1.call-done = bf16[3072,768]{1,0:T(8,128)(2,1)} async-done(((bf16[192,768]{1,0:T(8,128)(2,1)}), bf16[3072,768]{1,0:T(8,128)(2,1)}) %all-gather.17.cloned.1.call-update) | async-done | bytes 4718608 | tf_op jit(solution)/shard_map/all_gather | solution.py:72
  381.0 64.5 %all-gather.15.cloned.1.call-done = bf16[512,3072]{0,1:T(8,128)(2,1)} async-done(((bf16[512,384]{0,1:T(8,128)(2,1)}), bf16[512,3072]{0,1:T(8,128)(2,1)}) %all-gather.15.cloned.1.call-update) | async-done | bytes 3145744 | tf_op jit(solution)/shard_map/all_gather | solution.py:71
  445.5 6.8 %multiply_convert_fusion = bf16[512,768]{1,0:T(8,128)(2,1)} fusion(bf16[512,3072]{0,1:T(8,128)(2,1)} %all-gather.15.cloned.1.call-done, bf16[3072,768]{1,0:T(8,128)(2,1)} %all-gather.17.cloned.1.call-done, f32[768]{0:T(1024)S(1)} %reduce.1), kind=kOutput, calls=%fused_computation.21 | convolution fusion | flops 2416705536 | bytes 8653824 | tf_op jit(solution)/shard_map/dot_general | solution.py:15
  452.4 0.0 copy-done.1
  (7 shorter events, 0.1 us)
Async XLA Ops:
  6.5 191.4 %copy-start = (s32[1,32]{1,0:T(1,128)S(1)}, s32[1,32]{1,0:T(1,128)}, u32[]{:S(2)}) copy-start(s32[1,32]{1,0:T(1,128)} %param.17) | copy-start | bytes 388
  6.5 174.1 %copy-start.6 = (f32[1,6144]{1,0:T(1,128)S(1)}, f32[1,6144]{1,0:T(1,128)}, u32[]{:S(2)}) copy-start(f32[1,6144]{1,0:T(1,128)} %param.13) | copy-start | bytes 73732
  6.5 94.5 %all-gather.7.cloned.1.call-start = ((), (), s32[]{:S(2)}) async-start(), calls=%async_computation | async-start | bytes 7077888 | tf_op jit(solution)/shard_map/all_gather | solution.py:22
  7.3 173.4 %all-gather.9.cloned.1.call-start = ((), (), s32[]{:S(2)}) async-start(), calls=%async_computation.1 | async-start | bytes 15040512 | tf_op jit(solution)/shard_map/all_gather | solution.py:29
  8.0 260.3 %all-gather.11.cloned.1.call-start = ((), (), s32[]{:S(2)}) async-start(), calls=%async_computation.2 | async-start | bytes 3538944 | tf_op jit(solution)/shard_map/all_gather | solution.py:45
  101.1 4.6 %copy-start.2 = (bf16[512,6144]{1,0:T(8,128)(2,1)S(1)}, bf16[512,6144]{1,0:T(8,128)(2,1)}, u32[]{:S(2)}) copy-start(bf16[512,6144]{1,0:T(8,128)(2,1)} %all-gather.7.cloned.1.call-done) | copy-start | bytes 18874372
  195.4 8.5 %copy-start.5 = (f32[3]{0:T(128)S(1)}, f32[3]{0:T(128)}, u32[]{:S(2)}) copy-start(f32[3]{0:T(128)} %param.16) | copy-start | bytes 40
  196.4 144.5 %all-gather.13.cloned.1.call-start = ((), (), s32[]{:S(2)}) async-start(), calls=%async_computation.3 | async-start | bytes 3538944 | tf_op jit(solution)/shard_map/all_gather | solution.py:46
  197.3 183.7 %all-gather.17.cloned.1.call-start = ((), (), s32[]{:S(2)}) async-start(), calls=%async_computation.5 | async-start | bytes 5013504 | tf_op jit(solution)/shard_map/all_gather | solution.py:72
  197.9 247.7 %all-gather.15.cloned.1.call-start = ((), (), s32[]{:S(2)}) async-start(), calls=%async_computation.4 | async-start | bytes 3538944 | tf_op jit(solution)/shard_map/all_gather | solution.py:71
  340.9 33.5 %copy-start.4 = (f32[1,768]{1,0:T(1,128)S(1)}, f32[1,768]{1,0:T(1,128)}, u32[]{:S(2)}) copy-start(f32[1,768]{1,0:T(1,128)} %param.15) | copy-start | bytes 9220
  340.9 15.0 %copy-start.3 = (bf16[4096,384]{0,1:T(8,128)(2,1)S(1)}, bf16[4096,384]{0,1:T(8,128)(2,1)}, u32[]{:S(2)}) copy-start(bf16[4096,384]{0,1:T(8,128)(2,1)} %get-tuple-element.18) | copy-start | bytes 9437188 | tf_op jit(solution)/shard_map/cond
  374.4 78.0 %copy-start.1 = (s32[1,32]{1,0:T(1,128)S(1)}, s32[1,32]{1,0:T(1,128)}, u32[]{:S(2)}) copy-start(s32[1,32]{1,0:T(1,128)} %param.17) | copy-start | bytes 388
Sparse Core Ops, SparseCore 0:
  9.7 91.3 all-gather.6
  102.8 77.8 all-gather.8
  196.6 71.7 all-gather.10
  269.8 71.0 all-gather.12
  342.5 38.4 all-gather.16
  383.2 62.3 all-gather.14
where the time goes:
time: 459 us
  waiting for transfers between devices  375 us (82%)
  matrix products  50.8 us (11%)
  other arithmetic  14.7 us (3%)
  between operations  14.1 us (3%)
    all_gather x1, waiting for transfers between devices, local(): x_panel = lax.all_gather(tokens, 'col', axis=1, tiled=True)  92.3 us
    all_gather x1, waiting for transfers between devices, local(): lax.all_gather(w_qkv, ('dp', 'row'), axis=0, tiled=True)  73.2 us
    all_gather x1, waiting for transfers between devices, local(): lax.all_gather(values_local, 'row', axis=0, tiled=True)  72.6 us
    all_gather x1, waiting for transfers between devices, local(): heads_all = lax.all_gather(attended, 'col', axis=1, tiled=True)  64.5 us
    all_gather x1, waiting for transfers between devices, local(): lax.all_gather(keys_local, 'row', axis=0, tiled=True)  64.3 us
    dot_general x2, matrix products, joint_fold(): return jnp.dot(left, piece, preferred_element_type=jnp.float32)  21.6 us
    dot_general x1, matrix products, compute(): jnp.einsum('thd,shd->hts', query, key_piece, preferred_element_type=jnp.f...  15 us
    dot_general x1, matrix products, compute(): jnp.einsum('hts,shd->thd', rounded, value_piece, preferred_element_type=j...  14.2 us
  transfers between devices with their start and end apart: 6, of which 6 were waited for; matrix products, arithmetic and copies ran while one was open for 10% of the time, Pallas kernels for 0%

commit v1 on v0

v1 whole, which is shorter than its diff:
```python
import math

import jax
import jax.numpy as jnp
from jax import lax
from jax.experimental import pallas as pl
from jax.experimental.pallas import tpu as pltpu
from jax.sharding import PartitionSpec as P

HD = 128
BLK = 128
EPS = 1e-06
FAR = 2048.0
F32 = jnp.float32
BF16 = jnp.bfloat16
MESH = pl.DeviceIdType.MESH
N_FLOWS = 136


class Net:
    def __init__(self, ss, rs):
        self.ss, self.rs, self.count, self.sent = ss, rs, 0, []

    def ids(self, amount):
        first = self.count
        self.count += amount
        assert self.count <= N_FLOWS
        return list(range(first, self.count))

    def copy(self, i, src, dst, device):
        return pltpu.make_async_remote_copy(
            src_ref=src,
            dst_ref=dst,
            send_sem=self.ss.at[i],
            recv_sem=self.rs.at[i],
            device_id=device,
            device_id_type=MESH,
        )

    def send(self, i, src, dst, device, keep=True):
        copy = self.copy(i, src, dst, device)
        copy.start()
        if keep:
            self.sent.append(copy)
        return copy

    def recv(self, i, ref, device):
        self.copy(i, ref, ref, device).wait_recv()


def kernel(
    tok, wq, wo, shift, scale, gate, gain, seg, out,
    G, Xg, kvx, qx, woG, attg, acc, oacc, bacc, mod, ast, st, segb, ss, rs, ls,
):
    d, row, c = lax.axis_index("dp"), lax.axis_index("row"), lax.axis_index("col")
    y, l = row // 2, row % 2
    h, z = c // 4, c % 4
    yn, yf, yb = (y + 1) % 4, (y + 2) % 4, (y + 3) % 4
    zn, zf, zb = (z + 1) % 4, (z + 2) % 4, (z + 3) % 4
    h2 = 1 - h
    core = (1 - d, row, c)
    xl = (d, 2 * y + 1 - l, c)
    yp, ym = (d, 2 * yn + l, c), (d, 2 * yb + l, c)
    zp, zm = (d, row, 4 * h + zn), (d, row, 4 * h + zb)
    xh = (d, row, 4 * h2 + z)
    sw = (l, 2 * y + d, c)
    rr = 2 * y + d
    net = Net(ss, rs)

    def both_sides(first, second):
        pl.when(d == l)(first)
        pl.when(d != l)(second)

    x = tok[...].astype(F32)
    part_mean = jnp.sum(x, axis=-1, keepdims=True) * (1.0 / 768.0)
    off = x - part_mean
    part_sq = jnp.sum(off * off, axis=-1, keepdims=True)
    lane = lax.broadcasted_iota(jnp.int32, (512, 128), 1)
    columns = jnp.where(lane == 0, part_mean, jnp.where(lane == 1, part_sq, 0.0))
    st[c] = columns.T[:8]
    for b in range(32):
        segb[0, b : b + 1, :] = jnp.full((1, 128), seg[0, b], jnp.int32).astype(F32)

    barrier = pltpu.get_barrier_semaphore()
    col_peers = [(d, row, (c + k) % 8) for k in range(1, 8)]
    for peer in col_peers + [core, xl, yp, ym]:
        pl.semaphore_signal(barrier, inc=1, device_id=peer, device_id_type=MESH)

    @pl.when(d != l)
    def _():
        pl.semaphore_signal(barrier, inc=1, device_id=sw, device_id_type=MESH)

    pl.semaphore_wait(barrier, 11 + (d + l) % 2)

    def wid(dd, yy, ll):
        return 8 * dd + 2 * yy + ll

    class Weight:
        def __init__(self, src, dst, rows, local_sem):
            self.src, self.dst, self.half = src, dst, rows // 2
            self.f = net.ids(17)
            self.local = pltpu.make_async_copy(src, dst.at[wid(d, y, l)], local_sem)

        def at(self, dd, yy, ll, part=None):
            ref = self.dst.at[wid(dd, yy, ll)]
            if part is None:
                return ref
            return ref.at[pl.ds(part * self.half, self.half)]

        def go(self, i, ref, device):
            net.send(self.f[i], ref, ref, device)

        def got(self, i, ref):
            net.recv(self.f[i], ref, core)

        def own(self):
            me = self.at(d, y, l)
            for i, device in ((1, yp), (2, ym), (0, xl), (3, core)):
                net.send(self.f[i], self.src, me, device)
            self.local.start()

        def first_ring(self):
            self.got(1, self.at(d, yb, l))
            self.go(7, self.at(d, yb, l, 0), yp)
            self.go(8, self.at(d, yb, l), core)
            self.got(2, self.at(d, yn, l))
            self.go(9, self.at(d, yn, l, 1), ym)
            self.go(10, self.at(d, yn, l), core)

        def pair(self):
            ref = self.at(d, y, 1 - l)
            self.got(0, ref)
            self.go(4, ref, yp)
            self.go(5, ref, ym)
            self.go(6, ref, core)

        def second_ring(self):
            self.got(4, self.at(d, yb, 1 - l))
            self.go(11, self.at(d, yb, 1 - l, 0), yp)
            self.go(12, self.at(d, yb, 1 - l), core)
            self.got(5, self.at(d, yn, 1 - l))
            self.go(13, self.at(d, yn, 1 - l, 1), ym)
            self.go(14, self.at(d, yn, 1 - l), core)

        def near(self):
            self.local.wait()
            self.got(3, self.at(1 - d, y, l))
            self.got(6, self.at(1 - d, y, 1 - l))
            self.got(8, self.at(1 - d, yb, l))
            self.got(10, self.at(1 - d, yn, l))
            self.got(12, self.at(1 - d, yb, 1 - l))
            self.got(14, self.at(1 - d, yn, 1 - l))

        def far(self):
            self.got(7, self.at(d, yf, l, 0))
            self.got(9, self.at(d, yf, l, 1))
            self.go(15, self.at(d, yf, l), core)
            self.got(11, self.at(d, yf, 1 - l, 0))
            self.got(13, self.at(d, yf, 1 - l, 1))
            self.go(16, self.at(d, yf, 1 - l), core)

        def rest(self):
            self.got(15, self.at(1 - d, yf, l))
            self.got(16, self.at(1 - d, yf, 1 - l))

    wqkv = Weight(wq, G, 384, ls.at[0])
    wout = Weight(wo, woG, 192, ls.at[1])
    wqkv.own()

    seg_id = net.ids(1)[0]
    net.send(seg_id, segb.at[0], segb.at[1], core)
    st_ids = net.ids(7)
    for k in range(1, 8):
        net.send(st_ids[k - 1], st.at[c], st.at[c], col_peers[k - 1])
    for k in range(1, 8):
        net.recv(st_ids[k - 1], st.at[(c + 8 - k) % 8], core)
    means = [st[k, 0:1, :] for k in range(8)]
    mean = sum(means) * 0.125
    total_sq = sum(st[k, 1:2, :] for k in range(8))
    total_sq = total_sq + 768.0 * sum((m - mean) * (m - mean) for m in means)
    inv = lax.rsqrt(total_sq * (1.0 / 6144.0) + EPS)
    sub = lax.broadcasted_iota(jnp.int32, (128, 512), 0)
    columns = jnp.where(sub == 0, mean, jnp.where(sub == 1, inv, 0.0)).T
    lanes = pl.ds(pl.multiple_of(c * 768, 768), 768)
    normed = (tok[...].astype(F32) - columns[:, 0:1]) * columns[:, 1:2]
    modulated = (normed * (1.0 + scale[0:1, lanes]) + shift[0:1, lanes]).astype(BF16)
    swap_ids = net.ids(2)
    halves = (pl.ds(0, 256), pl.ds(256, 256))

    def keep_x():
        Xg[c] = modulated

    def swap_x():
        mod[...] = modulated
        for p in range(2):
            net.send(swap_ids[p], mod.at[halves[p]], Xg.at[c, halves[p]], sw, keep=False)

    both_sides(keep_x, swap_x)

    net.recv(seg_id, segb.at[1], core)
    slot = jnp.where(d == l, 0, 1)
    lane_row = lax.broadcasted_iota(jnp.int32, (1, 128), 1).astype(F32)

    def fill(b, carry):
        code = segb[slot, pl.ds(b, 1), :]
        other = jnp.where(lane_row == code, 0.0, 1.0).astype(BF16)
        tile = jnp.broadcast_to(other, (128, 128))
        ones = jnp.ones((128, 128), BF16)
        rows = pl.ds(pl.multiple_of((b % 4) * 128, 128), 128)
        for j in range(3):
            kvx[j, b // 4, rows, 384:512] = tile
            kvx[j, b // 4, rows, 0:128] = ones
        return carry

    def fill_q(b, carry):
        code = segb[slot, pl.ds(4 * rr + b, 1), :]
        same = jnp.where(lane_row == code, -FAR, 0.0).astype(BF16)
        tile = jnp.broadcast_to(same, (128, 128))
        rows = pl.ds(pl.multiple_of(b * 128, 128), 128)
        for j in range(3):
            qx[j, rows, 128:256] = tile
        return carry

    def wait_swap_x():
        for p in range(2):
            net.recv(swap_ids[p], Xg.at[c, halves[p]], sw)

    pl.when(d != l)(wait_swap_x)

    xi = net.ids(14)

    def xat(hh, zz, p):
        return Xg.at[4 * hh + zz, halves[p]]

    def xgo(i, ref, device):
        net.send(xi[i], ref, ref, device)

    def xgot(i, ref):
        net.recv(xi[i], ref, core)

    xgo(2, xat(h, z, 0), zp)
    xgo(5, xat(h, z, 1), zm)
    xgo(0, xat(h, z, 0), xh)
    xgo(1, xat(h, z, 1), xh)
    xgo(3, xat(h, z, 1), zp)
    xgo(4, xat(h, z, 0), zm)

    lax.fori_loop(0, 32, fill, 0)
    lax.fori_loop(0, 4, fill_q, 0)

    wqkv.first_ring()
    xgot(2, xat(h, zb, 0))
    xgo(6, xat(h, zb, 0), zp)
    xgot(5, xat(h, zn, 1))
    xgo(7, xat(h, zn, 1), zm)
    wqkv.pair()
    xgot(0, xat(h2, z, 0))
    xgo(8, xat(h2, z, 0), zp)
    xgo(10, xat(h2, z, 0), zm)
    xgot(1, xat(h2, z, 1))
    xgo(11, xat(h2, z, 1), zm)
    xgo(9, xat(h2, z, 1), zp)
    wqkv.second_ring()
    xgot(8, xat(h2, zb, 0))
    xgo(12, xat(h2, zb, 0), zp)
    xgot(11, xat(h2, zn, 1))
    xgo(13, xat(h2, zn, 1), zm)

    a0 = yf
    delta = (zf + 4 - yf) % 4
    third = jnp.where(delta == 0, 1, delta)
    e0 = (a0 + jnp.where(third == 1, 2, 1)) % 4
    e1 = (a0 + jnp.where(third == 3, 2, 3)) % 4
    e2 = (a0 + third) % 4

    def product(block, j):
        left = Xg[block]
        cols = slice(384 * j, 384 * (j + 1))
        right = jnp.concatenate([G[2 * block, :, cols], G[2 * block + 1, :, cols]], axis=0)
        return jnp.dot(left, right, preferred_element_type=F32)

    acc[...] = jnp.zeros_like(acc)
    wqkv.near()
    for i, hh, zz, p in ((3, h, zb, 1), (4, h, zn, 0), (9, h2, zb, 1), (10, h2, zn, 0)):
        xgot(i, xat(hh, zz, p))

    def early(s, carry):
        block = 4 * (s % 2) + jnp.where(s < 2, e0, e1)
        for j in range(3):
            acc[j] += product(block, j)
        return carry

    lax.fori_loop(0, 4, early, 0)
    wqkv.far()
    wout.own()
    xgot(6, xat(h, zf, 0))
    xgot(7, xat(h, zf, 1))
    xgot(12, xat(h2, zf, 0))
    xgot(13, xat(h2, zf, 1))
    wqkv.rest()

    def rms(v):
        return v * lax.rsqrt(jnp.mean(v * v, axis=-1, keepdims=True) + EPS)

    def finish(j):
        def late(s, carry):
            block = 4 * (s % 2) + jnp.where(s < 2, e2, a0)
            acc[j] += product(block, j)
            return carry

        lax.fori_loop(0, 4, late, 0)
        qx[j, :, 0:128] = (rms(acc[j, :, 0:128]) * gain[j]).astype(BF16)
        kvx[j, rr, :, 256:384] = rms(acc[j, :, 128:256]).astype(BF16)
        kvx[j, rr, :, 128:256] = acc[j, :, 256:384].astype(BF16)

    ki = [net.ids(8) for _ in range(3)]

    def kat(j, yy, dd, p=None):
        rows = pl.ds(0, 512) if p is None else halves[p]
        return kvx.at[j, 2 * yy + dd, rows, pl.ds(128, 256)]

    def kgo(j, i, ref, device):
        net.send(ki[j][i], ref, ref, device)

    def kgot(j, i, ref):
        net.recv(ki[j][i], ref, core)

    def kv_own(j):
        me = kat(j, y, d)
        kgo(j, 0, me, yp)
        kgo(j, 1, me, ym)
        kgo(j, 2, me, core)

    def kv_forward(j):
        kgot(j, 0, kat(j, yb, d))
        kgo(j, 3, kat(j, yb, d, 0), yp)
        kgo(j, 4, kat(j, yb, d), core)
        kgot(j, 1, kat(j, yn, d))
        kgo(j, 5, kat(j, yn, d, 1), ym)
        kgo(j, 6, kat(j, yn, d), core)

    def kv_far(j):
        kgot(j, 3, kat(j, yf, d, 0))
        kgot(j, 5, kat(j, yf, d, 1))
        kgo(j, 7, kat(j, yf, d), core)

    power = (1.0 / HD**0.5) * math.log2(math.e)

    def attend(j, amount, row_of):
        def step(s, carry):
            key_row = row_of(s // 2)
            rows = pl.ds(pl.multiple_of((s % 2) * 256, 256), 256)

            @pl.when(jnp.abs(key_row - rr) <= 4)
            def _():
                scores = lax.dot_general(
                    qx[j, rows, :],
                    kvx[j, key_row, :, 256:512],
                    (((1,), (1,)), ((), ())),
                    preferred_element_type=F32,
                )
                weights = jnp.exp2(scores * power).astype(BF16)
                oacc[rows, :] += jnp.dot(
                    weights, kvx[j, key_row, :, 0:256], preferred_element_type=F32
                )

            return carry

        lax.fori_loop(0, 2 * amount, step, 0)

    def attend_here(j):
        oacc[...] = jnp.zeros_like(oacc)
        kgot(j, 2, kat(j, y, 1 - d))
        attend(j, 2, lambda k: 2 * y + k)

    def attend_near(j):
        kgot(j, 4, kat(j, yb, 1 - d))
        kgot(j, 6, kat(j, yn, 1 - d))
        attend(j, 4, lambda k: 2 * ((y + 3 + 2 * (k // 2)) % 4) + k % 2)

    def attend_far(j):
        kgot(j, 7, kat(j, yf, 1 - d))
        attend(j, 2, lambda k: 2 * yf + k)

    ai = [net.ids(10) for _ in range(3)]

    def aat(j, hh, zz, p=None):
        ref = attg.at[j, 4 * hh + zz]
        return ref if p is None else ref.at[halves[p]]

    def ago(j, i, ref, device):
        net.send(ai[j][i], ref, ref, device)

    def agot(j, i, ref):
        net.recv(ai[j][i], ref, core)

    def att_put(j):
        value = (oacc[:, 128:256] / oacc[:, 0:128]).astype(BF16)

        def keep():
            attg[j, c] = value

        def swap():
            ast[j] = value
            net.send(ai[j][9], ast.at[j], attg.at[j, c], sw, keep=False)

        both_sides(keep, swap)

    def att_own(j):
        pl.when(d != l)(lambda: net.recv(ai[j][9], attg.at[j, c], sw))
        me = aat(j, h, z)
        ago(j, 0, me, xh)
        ago(j, 1, me, zp)
        ago(j, 2, me, zm)

    def att_forward(j):
        agot(j, 1, aat(j, h, zb))
        ago(j, 3, aat(j, h, zb, 0), zp)
        agot(j, 2, aat(j, h, zn))
        ago(j, 4, aat(j, h, zn, 1), zm)
        agot(j, 0, aat(j, h2, z))
        ago(j, 5, aat(j, h2, z), zp)
        ago(j, 6, aat(j, h2, z), zm)

    def att_second(j):
        agot(j, 5, aat(j, h2, zb))
        ago(j, 7, aat(j, h2, zb, 0), zp)
        agot(j, 6, aat(j, h2, zn))
        ago(j, 8, aat(j, h2, zn, 1), zm)

    def att_rest(j):
        agot(j, 3, aat(j, h, zf, 0))
        agot(j, 4, aat(j, h, zf, 1))
        agot(j, 7, aat(j, h2, zf, 0))
        agot(j, 8, aat(j, h2, zf, 1))

    def wrows(block, j):
        pieces = []
        for e in range(2):
            unit = 6 * block + 2 * j + e
            pieces.append(woG[unit // 3, pl.ds(pl.multiple_of((unit % 3) * 64, 64), 64), :])
        return pieces

    def project_out(j):
        def step(p, carry):
            left = jnp.concatenate([attg[j, 2 * p], attg[j, 2 * p + 1]], axis=1)
            right = jnp.concatenate(wrows(2 * p, j) + wrows(2 * p + 1, j), axis=0)
            bacc[...] += jnp.dot(left, right, preferred_element_type=F32)
            return carry

        lax.fori_loop(0, 4, step, 0)

    finish(0)
    kv_own(0)
    finish(1)
    finish(2)
    attend_here(0)
    kv_forward(0)
    kv_own(1)
    attend_near(0)
    kv_far(0)
    attend_far(0)
    att_put(0)
    kv_forward(1)
    kv_own(2)
    att_own(0)
    attend_here(1)
    attend_near(1)
    att_forward(0)
    kv_far(1)
    attend_far(1)
    att_put(1)
    kv_forward(2)
    att_own(1)
    att_second(0)
    wout.pair()
    wout.first_ring()
    attend_here(2)
    attend_near(2)
    kv_far(2)
    att_forward(1)
    attend_far(2)
    att_put(2)
    att_own(2)
    wout.second_ring()
    att_second(1)
    bacc[...] = jnp.zeros_like(bacc)
    att_forward(2)
    wout.far()
    att_rest(0)
    wout.near()
    wout.rest()
    project_out(0)
    att_second(2)
    att_rest(1)
    project_out(1)
    att_rest(2)
    project_out(2)
    out[...] = (gate[...] * bacc[...]).astype(BF16)

    for copy in net.sent:
        copy.wait_send()

    @pl.when(d != l)
    def _():
        for p in range(2):
            net.copy(swap_ids[p], mod.at[halves[p]], Xg.at[c, halves[p]], sw).wait_send()
        for j in range(3):
            net.copy(ai[j][9], ast.at[j], attg.at[j, c], sw).wait_send()


def local(tokens, w_qkv, w_out, ada_shift, ada_scale, out_gate, head_gain, block_segment):
    vmem = pl.BlockSpec(memory_space=pltpu.VMEM)
    smem = pl.BlockSpec(memory_space=pltpu.SMEM)
    return pl.pallas_call(
        kernel,
        out_shape=jax.ShapeDtypeStruct((512, 768), BF16),
        in_specs=[vmem] * 6 + [smem] * 2,
        out_specs=vmem,
        scratch_shapes=[
            pltpu.VMEM((16, 384, 1152), BF16),
            pltpu.VMEM((8, 512, 768), BF16),
            pltpu.VMEM((3, 8, 512, 512), BF16),
            pltpu.VMEM((3, 512, 256), BF16),
            pltpu.VMEM((16, 192, 768), BF16),
            pltpu.VMEM((3, 8, 512, 128), BF16),
            pltpu.VMEM((3, 512, 384), F32),
            pltpu.VMEM((512, 256), F32),
            pltpu.VMEM((512, 768), F32),
            pltpu.VMEM((512, 768), BF16),
            pltpu.VMEM((3, 512, 128), BF16),
            pltpu.VMEM((8, 8, 512), F32),
            pltpu.VMEM((2, 32, 128), F32),
            pltpu.SemaphoreType.DMA((N_FLOWS,)),
            pltpu.SemaphoreType.DMA((N_FLOWS,)),
            pltpu.SemaphoreType.DMA((2,)),
        ],
        compiler_params=pltpu.CompilerParams(
            collective_id=0, has_side_effects=True, vmem_limit_bytes=60 * 2**20
        ),
    )(tokens, w_qkv, w_out, ada_shift, ada_scale, out_gate, head_gain, block_segment)


def solution(mesh):
    placed = (
        P(("dp", "row"), "col"),
        P(("dp", "row"), "col"),
        P(("dp", "row"), "col"),
        P("dp", None),
        P("dp", None),
        P("dp", "col"),
        P("col"),
        P("dp", None),
    )
    return jax.shard_map(
        local, mesh=mesh, in_specs=placed, out_specs=P(("dp", "row"), "col"), check_vma=False
    )
```

time: 459 us -> 156 us (0.34)
  waiting for transfers between devices: 375 us -> 0 us
  Pallas kernels: 0 us -> 152 us
  matrix products: 50.8 us -> 0 us
  other arithmetic: 14.7 us -> 0 us
  between operations: 14.1 us -> 0.01 us
    all_gather x6 -> x0, waiting for transfers between devices: 373 us -> none  [the longest x1 92.3 us: local(): x_panel = lax.all_gather(tokens, 'col', axis=1, tiled=True)]
    pallas_call x0 -> x1, Pallas kernels: none -> 152 us  [local(): pl.pallas_call(kernel, out_shape=jax.ShapeDtypeStruct((512, 768), BF16),...]
    dot_general x4 -> x0, matrix products: 50.8 us -> none  [the longest x2 21.6 us: joint_fold(): return jnp.dot(left, piece, preferred_element_type=jnp.float32)]
    convert_element_type x4 -> x0, other arithmetic: 8.08 us -> none  [the longest x1 5.15 us: local(): (query_segment[:, None] == token_segment[None, :]).astype(jnp.float32)]
    reduce_sum x4 -> x0, other arithmetic: 5.8 us -> none  [the longest x1 3.84 us: local(): row_mean = jnp.mean(x_float, axis=-1, keepdims=True)]
  transfers between devices with their start and end apart: 6 -> 0, of which waited for: 6 -> 0; matrix products, arithmetic and copies ran while one was open for 10% -> 0% of each run, Pallas kernels for 0% -> 0%
where the time goes in v1:
time: 156 us; the launch traced here: 154 us
  Pallas kernels  152 us (97%)
  local copies, waits for them, and re-layouts  2.06 us (1%)
    pallas_call x1, Pallas kernels, local(): pl.pallas_call(kernel, out_shape=jax.ShapeDtypeStruct((512, 768), BF16),...  152 us

profile of v1, /device:TPU:1, one launch (start us, length us, event | category | flops | bytes accessed | tf_op | source)
XLA Modules:
  0.0 153.6 jit_solution(5586486409040191515)
XLA Ops:
  0.0 151.5 %shard_map.82 = bf16[512,768]{1,0:T(8,128)(2,1)} custom-call(bf16[512,768]{1,0:T(8,128)(2,1)} %tok.1, bf16[384,1152]{1,0:T(8,128)(2,1)} %wq.1, bf16[192,768]{1,0:T(8,128)(2,1)} %wo.1, f32[1,6144]{1,0:T(1,128)} %shift.1, f32[1,6144]{1,0:T(1,128)} %scale.1, f32[1,768]{1,0:T(1,128)} %gate.1, f32[3]{0:T(128)} %gain.1, s32[1,32]{1,0:T(1,128)} %seg.1), custom_call_target="tpu_custom_call" | custom-call | tf_op jit(solution)/shard_map/pallas_call | solution.py:515
  151.5 2.1 %copy.10 = bf16[512,768]{1,0:T(8,128)(2,1)} copy(bf16[512,768]{1,0:T(8,128)(2,1)} %shard_map.82) | data formatting | bytes 1572864

commit v2 on v1

--- a/solution.py
+++ b/solution.py
@@ -44,13 +44,16 @@
             self.sent.append(copy)
         return copy
 
+    def add(self, i, src, dst, device):
+        self.sent.append(self.copy(i, src, dst, device))
+
     def recv(self, i, ref, device):
         self.copy(i, ref, ref, device).wait_recv()
 
 
 def kernel(
-    tok, wq, wo, shift, scale, gate, gain, seg, out,
-    G, Xg, kvx, qx, woG, attg, acc, oacc, bacc, mod, ast, st, segb, ss, rs, ls,
+    tok_hbm, wq, wo, shift, scale, gate, gain, seg, out,
+    tok, G, Xg, kvx, qx, woG, attg, acc, oacc, bacc, mod, ast, st, segb, ss, rs, ls,
 ):
     d, row, c = lax.axis_index("dp"), lax.axis_index("row"), lax.axis_index("col")
     y, l = row // 2, row % 2
@@ -71,6 +74,132 @@
         pl.when(d == l)(first)
         pl.when(d != l)(second)
 
+    barrier = pltpu.get_barrier_semaphore()
+    col_peers = [(d, row, (c + k) % 8) for k in range(1, 8)]
+    for peer in col_peers + [core, xl, yp, ym]:
+        pl.semaphore_signal(barrier, inc=1, device_id=peer, device_id_type=MESH)
+
+    @pl.when(d != l)
+    def _():
+        pl.semaphore_signal(barrier, inc=1, device_id=sw, device_id_type=MESH)
+
+    tok_copy = pltpu.make_async_copy(tok_hbm, tok, ls.at[2])
+    tok_copy.start()
+    pl.semaphore_wait(barrier, 11 + (d + l) % 2)
+
+    def wid(dd, yy, ll):
+        return 8 * dd + 2 * yy + ll
+
+    class Weight:
+        def __init__(self, src, dst, rows, local_sem):
+            self.src, self.dst, self.half = src, dst, rows // 2
+            self.f = net.ids(17)
+            self.local = pltpu.make_async_copy(src, dst.at[wid(d, y, l)], local_sem)
+
+        def at(self, dd, yy, ll, part=None):
+            ref = self.dst.at[wid(dd, yy, ll)]
+            if part is None:
+                return ref
+            return ref.at[pl.ds(part * self.half, self.half)]
+
+        def go(self, i, ref, device):
+            net.send(self.f[i], ref, ref, device)
+
+        def got(self, i, ref):
+            net.recv(self.f[i], ref, core)
+
+        def own(self):
+            me = self.at(d, y, l)
+            for i, device in ((1, yp), (2, ym), (0, xl), (3, core)):
+                net.send(self.f[i], self.src, me, device)
+            self.local.start()
+
+        def first_ring(self):
+            self.got(1, self.at(d, yb, l))
+            self.go(7, self.at(d, yb, l, 0), yp)
+            self.go(8, self.at(d, yb, l), core)
+            self.got(2, self.at(d, yn, l))
+            self.go(9, self.at(d, yn, l, 1), ym)
+            self.go(10, self.at(d, yn, l), core)
+
+        def pair(self):
+            ref = self.at(d, y, 1 - l)
+            self.got(0, ref)
+            send_xh()
+            self.go(4, ref, yp)
+            self.go(5, ref, ym)
+            self.go(6, ref, core)
+
+        def second_ring(self):
+            self.got(4, self.at(d, yb, 1 - l))
+            self.go(11, self.at(d, yb, 1 - l, 0), yp)
+            self.go(12, self.at(d, yb, 1 - l), core)
+            self.got(5, self.at(d, yn, 1 - l))
+            self.go(13, self.at(d, yn, 1 - l, 1), ym)
+            self.go(14, self.at(d, yn, 1 - l), core)
+
+        def near(self):
+            self.local.wait()
+            self.got(3, self.at(1 - d, y, l))
+            self.got(6, self.at(1 - d, y, 1 - l))
+            self.got(8, self.at(1 - d, yb, l))
+            self.got(10, self.at(1 - d, yn, l))
+            self.got(12, self.at(1 - d, yb, 1 - l))
+            self.got(14, self.at(1 - d, yn, 1 - l))
+
+        def far(self):
+            self.got(7, self.at(d, yf, l, 0))
+            self.got(9, self.at(d, yf, l, 1))
+            self.go(15, self.at(d, yf, l), core)
+            self.got(11, self.at(d, yf, 1 - l, 0))
+            self.got(13, self.at(d, yf, 1 - l, 1))
+            self.go(16, self.at(d, yf, 1 - l), core)
+
+        def rest(self):
+            self.got(15, self.at(1 - d, yf, l))
+            self.got(16, self.at(1 - d, yf, 1 - l))
+
+    class LateWeight(Weight):
+        def own(self):
+            me = self.at(d, y, l)
+            for i, device in ((1, yp), (2, ym), (0, xl), (3, core)):
+                net.send(self.f[i], self.src, me, device)
+            self.local.start()
+
+        def first_ring(self):
+            for i, yy, part, device in ((1, yb, 0, yp), (2, yn, 1, ym)):
+                self.got(i, self.at(d, yy, l))
+                self.go(3 + i, self.at(d, yy, l, part), device)
+                self.go(5 + i, self.at(d, yy, l), xl)
+                self.go(7 + i, self.at(d, yy, l), core)
+
+        def second_ring(self):
+            self.got(4, self.at(d, yf, l, 0))
+            self.got(5, self.at(d, yf, l, 1))
+            self.go(10, self.at(d, yf, l), xl)
+            self.go(11, self.at(d, yf, l), core)
+
+        def pair(self):
+            for i, yy, j in ((0, y, 12), (6, yb, 13), (7, yn, 14)):
+                self.got(i, self.at(d, yy, 1 - l))
+                self.go(j, self.at(d, yy, 1 - l), core)
+
+        def far(self):
+            self.got(10, self.at(d, yf, 1 - l))
+            self.go(15, self.at(d, yf, 1 - l), core)
+
+        def rest(self):
+            self.local.wait()
+            for i, yy, ll in ((3, y, l), (8, yb, l), (9, yn, l), (11, yf, l)):
+                self.got(i, self.at(1 - d, yy, ll))
+            for i, yy in ((12, y), (13, yb), (14, yn), (15, yf)):
+                self.got(i, self.at(1 - d, yy, 1 - l))
+
+    wqkv = Weight(wq, G, 384, ls.at[0])
+    wout = LateWeight(wo, woG, 192, ls.at[1])
+    wqkv.own()
+    tok_copy.wait()
+
     x = tok[...].astype(F32)
     part_mean = jnp.sum(x, axis=-1, keepdims=True) * (1.0 / 768.0)
     off = x - part_mean
@@ -81,91 +210,6 @@
     for b in range(32):
         segb[0, b : b + 1, :] = jnp.full((1, 128), seg[0, b], jnp.int32).astype(F32)
 
-    barrier = pltpu.get_barrier_semaphore()
-    col_peers = [(d, row, (c + k) % 8) for k in range(1, 8)]
-    for peer in col_peers + [core, xl, yp, ym]:
-        pl.semaphore_signal(barrier, inc=1, device_id=peer, device_id_type=MESH)
-
-    @pl.when(d != l)
-    def _():
-        pl.semaphore_signal(barrier, inc=1, device_id=sw, device_id_type=MESH)
-
-    pl.semaphore_wait(barrier, 11 + (d + l) % 2)
-
-    def wid(dd, yy, ll):
-        return 8 * dd + 2 * yy + ll
-
-    class Weight:
-        def __init__(self, src, dst, rows, local_sem):
-            self.src, self.dst, self.half = src, dst, rows // 2
-            self.f = net.ids(17)
-            self.local = pltpu.make_async_copy(src, dst.at[wid(d, y, l)], local_sem)
-
-        def at(self, dd, yy, ll, part=None):
-            ref = self.dst.at[wid(dd, yy, ll)]
-            if part is None:
-                return ref
-            return ref.at[pl.ds(part * self.half, self.half)]
-
-        def go(self, i, ref, device):
-            net.send(self.f[i], ref, ref, device)
-
-        def got(self, i, ref):
-            net.recv(self.f[i], ref, core)
-
-        def own(self):
-            me = self.at(d, y, l)
-            for i, device in ((1, yp), (2, ym), (0, xl), (3, core)):
-                net.send(self.f[i], self.src, me, device)
-            self.local.start()
-
-        def first_ring(self):
-            self.got(1, self.at(d, yb, l))
-            self.go(7, self.at(d, yb, l, 0), yp)
-            self.go(8, self.at(d, yb, l), core)
-            self.got(2, self.at(d, yn, l))
-            self.go(9, self.at(d, yn, l, 1), ym)
-            self.go(10, self.at(d, yn, l), core)
-
-        def pair(self):
-            ref = self.at(d, y, 1 - l)
-            self.got(0, ref)
-            self.go(4, ref, yp)
-            self.go(5, ref, ym)
-            self.go(6, ref, core)
-
-        def second_ring(self):
-            self.got(4, self.at(d, yb, 1 - l))
-            self.go(11, self.at(d, yb, 1 - l, 0), yp)
-            self.go(12, self.at(d, yb, 1 - l), core)
-            self.got(5, self.at(d, yn, 1 - l))
-            self.go(13, self.at(d, yn, 1 - l, 1), ym)
-            self.go(14, self.at(d, yn, 1 - l), core)
-
-        def near(self):
-            self.local.wait()
-            self.got(3, self.at(1 - d, y, l))
-            self.got(6, self.at(1 - d, y, 1 - l))
-            self.got(8, self.at(1 - d, yb, l))
-            self.got(10, self.at(1 - d, yn, l))
-            self.got(12, self.at(1 - d, yb, 1 - l))
-            self.got(14, self.at(1 - d, yn, 1 - l))
-
-        def far(self):
-            self.got(7, self.at(d, yf, l, 0))
-            self.got(9, self.at(d, yf, l, 1))
-            self.go(15, self.at(d, yf, l), core)
-            self.got(11, self.at(d, yf, 1 - l, 0))
-            self.got(13, self.at(d, yf, 1 - l, 1))
-            self.go(16, self.at(d, yf, 1 - l), core)
-
-        def rest(self):
-            self.got(15, self.at(1 - d, yf, l))
-            self.got(16, self.at(1 - d, yf, 1 - l))
-
-    wqkv = Weight(wq, G, 384, ls.at[0])
-    wout = Weight(wo, woG, 192, ls.at[1])
-    wqkv.own()
 
     seg_id = net.ids(1)[0]
     net.send(seg_id, segb.at[0], segb.at[1], core)
@@ -232,28 +276,36 @@
     def xat(hh, zz, p):
         return Xg.at[4 * hh + zz, halves[p]]
 
-    def xgo(i, ref, device):
-        net.send(xi[i], ref, ref, device)
+    def xgo(i, ref, device, keep=True):
+        net.send(xi[i], ref, ref, device, keep)
 
     def xgot(i, ref):
         net.recv(xi[i], ref, core)
 
+    def send_xh():
+        xgo(0, xat(h, z, 0), xh)
+        xgo(1, xat(h, z, 1), xh)
+
     xgo(2, xat(h, z, 0), zp)
     xgo(5, xat(h, z, 1), zm)
-    xgo(0, xat(h, z, 0), xh)
-    xgo(1, xat(h, z, 1), xh)
     xgo(3, xat(h, z, 1), zp)
     xgo(4, xat(h, z, 0), zm)
 
     lax.fori_loop(0, 32, fill, 0)
     lax.fori_loop(0, 4, fill_q, 0)
 
+    def x_forward():
+        xgot(2, xat(h, zb, 0))
+        xgo(6, xat(h, zb, 0), zp, None)
+        xgot(5, xat(h, zn, 1))
+        xgo(7, xat(h, zn, 1), zm, None)
+
+    pl.when(d == l)(x_forward)
     wqkv.first_ring()
-    xgot(2, xat(h, zb, 0))
-    xgo(6, xat(h, zb, 0), zp)
-    xgot(5, xat(h, zn, 1))
-    xgo(7, xat(h, zn, 1), zm)
     wqkv.pair()
+    pl.when(d != l)(x_forward)
+    net.add(xi[6], xat(h, zb, 0), xat(h, zb, 0), zp)
+    net.add(xi[7], xat(h, zn, 1), xat(h, zn, 1), zm)
     xgot(0, xat(h2, z, 0))
     xgo(8, xat(h2, z, 0), zp)
     xgo(10, xat(h2, z, 0), zm)
@@ -452,13 +504,16 @@
 
     finish(0)
     kv_own(0)
+    wout.first_ring()
     finish(1)
     finish(2)
+    wout.second_ring()
     attend_here(0)
     kv_forward(0)
     kv_own(1)
     attend_near(0)
     kv_far(0)
+    wout.pair()
     attend_far(0)
     att_put(0)
     kv_forward(1)
@@ -473,8 +528,7 @@
     kv_forward(2)
     att_own(1)
     att_second(0)
-    wout.pair()
-    wout.first_ring()
+    wout.far()
     attend_here(2)
     attend_near(2)
     kv_far(2)
@@ -482,18 +536,15 @@
     attend_far(2)
     att_put(2)
     att_own(2)
-    wout.second_ring()
     att_second(1)
     bacc[...] = jnp.zeros_like(bacc)
-    att_forward(2)
-    wout.far()
     att_rest(0)
-    wout.near()
     wout.rest()
     project_out(0)
-    att_second(2)
+    att_forward(2)
     att_rest(1)
     project_out(1)
+    att_second(2)
     att_rest(2)
     project_out(2)
     out[...] = (gate[...] * bacc[...]).astype(BF16)
@@ -512,12 +563,14 @@
 def local(tokens, w_qkv, w_out, ada_shift, ada_scale, out_gate, head_gain, block_segment):
     vmem = pl.BlockSpec(memory_space=pltpu.VMEM)
     smem = pl.BlockSpec(memory_space=pltpu.SMEM)
+    anyw = pl.BlockSpec(memory_space=pl.ANY)
     return pl.pallas_call(
         kernel,
         out_shape=jax.ShapeDtypeStruct((512, 768), BF16),
-        in_specs=[vmem] * 6 + [smem] * 2,
+        in_specs=[anyw] * 3 + [vmem] * 3 + [smem] * 2,
         out_specs=vmem,
         scratch_shapes=[
+            pltpu.VMEM((512, 768), BF16),
             pltpu.VMEM((16, 384, 1152), BF16),
             pltpu.VMEM((8, 512, 768), BF16),
             pltpu.VMEM((3, 8, 512, 512), BF16),
@@ -533,7 +586,7 @@
             pltpu.VMEM((2, 32, 128), F32),
             pltpu.SemaphoreType.DMA((N_FLOWS,)),
             pltpu.SemaphoreType.DMA((N_FLOWS,)),
-            pltpu.SemaphoreType.DMA((2,)),
+            pltpu.SemaphoreType.DMA((3,)),
         ],
         compiler_params=pltpu.CompilerParams(
             collective_id=0, has_side_effects=True, vmem_limit_bytes=60 * 2**20

time: 156 us -> 161 us (1.032)
  Pallas kernels: 152 us -> 156 us
    pallas_call x1, Pallas kernels: 152 us -> 156 us  [local(): pl.pallas_call(kernel, out_shape=jax.ShapeDtypeStruct((512, 768), BF16),...]
where the time goes in v2:
time: 161 us; the launch traced here: 158 us
  Pallas kernels  156 us (97%)
  local copies, waits for them, and re-layouts  2.06 us (1%)
    pallas_call x1, Pallas kernels, local(): pl.pallas_call(kernel, out_shape=jax.ShapeDtypeStruct((512, 768), BF16),...  156 us

profile of v2, /device:TPU:1, one launch (start us, length us, event | category | flops | bytes accessed | tf_op | source)
XLA Modules:
  0.0 158.1 jit_solution(6253745136221439304)
XLA Ops:
  0.0 156.0 %shard_map.82 = bf16[512,768]{1,0:T(8,128)(2,1)} custom-call(bf16[512,768]{1,0:T(8,128)(2,1)} %tok_hbm.1, bf16[384,1152]{1,0:T(8,128)(2,1)} %wq.1, bf16[192,768]{1,0:T(8,128)(2,1)} %wo.1, f32[1,6144]{1,0:T(1,128)} %shift.1, f32[1,6144]{1,0:T(1,128)} %scale.1, f32[1,768]{1,0:T(1,128)} %gate.1, f32[3]{0:T(128)} %gain.1, s32[1,32]{1,0:T(1,128)} %seg.1), custom_call_target="tpu_custom_call" | custom-call | tf_op jit(solution)/shard_map/pallas_call | solution.py:567
  156.0 2.1 %copy.10 = bf16[512,768]{1,0:T(8,128)(2,1)} copy(bf16[512,768]{1,0:T(8,128)(2,1)} %shard_map.82) | data formatting | bytes 1572864

commit v3 on v1

--- a/solution.py
+++ b/solution.py
@@ -14,12 +14,12 @@
 F32 = jnp.float32
 BF16 = jnp.bfloat16
 MESH = pl.DeviceIdType.MESH
-N_FLOWS = 136
+N_FLOWS = 128
 
 
 class Net:
     def __init__(self, ss, rs):
-        self.ss, self.rs, self.count, self.sent = ss, rs, 0, []
+        self.ss, self.rs, self.count, self.sent = ss, rs, 0, {}
 
     def ids(self, amount):
         first = self.count
@@ -37,20 +37,17 @@
             device_id_type=MESH,
         )
 
-    def send(self, i, src, dst, device, keep=True):
-        copy = self.copy(i, src, dst, device)
-        copy.start()
-        if keep:
-            self.sent.append(copy)
-        return copy
+    def send(self, i, src, dst, device, like, some=False):
+        self.copy(i, src, dst, device).start()
+        self.sent[i] = (like, some)
 
     def recv(self, i, ref, device):
         self.copy(i, ref, ref, device).wait_recv()
 
 
 def kernel(
-    tok, wq, wo, shift, scale, gate, gain, seg, out,
-    G, Xg, kvx, qx, woG, attg, acc, oacc, bacc, mod, ast, st, segb, ss, rs, ls,
+    tok_hbm, wq, wo, shift, scale, gate, gain, seg, out,
+    tok, G, Xg, kvx, qx, woG, attg, acc, oacc, bacc, mod, ast, st, segb, ss, rs, ls,
 ):
     d, row, c = lax.axis_index("dp"), lax.axis_index("row"), lax.axis_index("col")
     y, l = row // 2, row % 2
@@ -71,6 +68,22 @@
         pl.when(d == l)(first)
         pl.when(d != l)(second)
 
+    tok_copy = pltpu.make_async_copy(tok_hbm, tok, ls.at[2])
+    tok_copy.start()
+
+    barrier = pltpu.get_barrier_semaphore()
+    col_peers = [(d, row, (c + k) % 8) for k in range(1, 8)]
+    for peer in col_peers + [core, xl, yp, ym]:
+        pl.semaphore_signal(barrier, inc=1, device_id=peer, device_id_type=MESH)
+
+    @pl.when(d != l)
+    def _():
+        pl.semaphore_signal(barrier, inc=1, device_id=sw, device_id_type=MESH)
+
+    for b in range(32):
+        segb[0, b : b + 1, :] = jnp.full((1, 128), seg[0, b], jnp.int32).astype(F32)
+
+    tok_copy.wait()
     x = tok[...].astype(F32)
     part_mean = jnp.sum(x, axis=-1, keepdims=True) * (1.0 / 768.0)
     off = x - part_mean
@@ -78,18 +91,6 @@
     lane = lax.broadcasted_iota(jnp.int32, (512, 128), 1)
     columns = jnp.where(lane == 0, part_mean, jnp.where(lane == 1, part_sq, 0.0))
     st[c] = columns.T[:8]
-    for b in range(32):
-        segb[0, b : b + 1, :] = jnp.full((1, 128), seg[0, b], jnp.int32).astype(F32)
-
-    barrier = pltpu.get_barrier_semaphore()
-    col_peers = [(d, row, (c + k) % 8) for k in range(1, 8)]
-    for peer in col_peers + [core, xl, yp, ym]:
-        pl.semaphore_signal(barrier, inc=1, device_id=peer, device_id_type=MESH)
-
-    @pl.when(d != l)
-    def _():
-        pl.semaphore_signal(barrier, inc=1, device_id=sw, device_id_type=MESH)
-
     pl.semaphore_wait(barrier, 11 + (d + l) % 2)
 
     def wid(dd, yy, ll):
@@ -98,80 +99,113 @@
     class Weight:
         def __init__(self, src, dst, rows, local_sem):
             self.src, self.dst, self.half = src, dst, rows // 2
-            self.f = net.ids(17)
+            self.parts = {None: pl.ds(0, rows), 0: pl.ds(0, rows // 2), 1: pl.ds(rows // 2, rows // 2)}
+            self.f = dict(zip(self.names, net.ids(len(self.names))))
             self.local = pltpu.make_async_copy(src, dst.at[wid(d, y, l)], local_sem)
 
+        names = (
+            "own_yp0", "own_yp1", "own_ym0", "own_ym1", "own_xl0", "own_xl1",
+            "own_core", "fwd_yp", "fwd_ym", "core_yb", "core_yn", "pair_yp0",
+            "pair_yp1", "pair_ym0", "pair_ym1", "core_pair", "last_yp", "last_ym",
+            "core_yb2", "core_yn2", "far0", "far1", "far2", "far3",
+        )
+
         def at(self, dd, yy, ll, part=None):
-            ref = self.dst.at[wid(dd, yy, ll)]
-            if part is None:
-                return ref
-            return ref.at[pl.ds(part * self.half, self.half)]
-
-        def go(self, i, ref, device):
-            net.send(self.f[i], ref, ref, device)
-
-        def got(self, i, ref):
-            net.recv(self.f[i], ref, core)
-
-        def own(self):
-            me = self.at(d, y, l)
-            for i, device in ((1, yp), (2, ym), (0, xl), (3, core)):
-                net.send(self.f[i], self.src, me, device)
+            return self.dst.at[wid(dd, yy, ll), self.parts[part]]
+
+        def go(self, name, device, dd, yy, ll, part=None, src=None):
+            ref = self.at(dd, yy, ll, part)
+            like = lambda: self.dst.at[0, self.parts[part]]
+            net.send(self.f[name], ref if src is None else src, ref, device, like)
+
+        def got(self, name, dd, yy, ll, part=None):
+            net.recv(self.f[name], self.at(dd, yy, ll, part), core)
+
+        def own(self, name, device, part=None):
+            self.go(name, device, d, y, l, part, self.src.at[self.parts[part]])
+
+        def own_y(self):
+            self.own("own_yp0", yp, 0)
+            self.own("own_ym1", ym, 1)
+            self.own("own_yp1", yp, 1)
+            self.own("own_ym0", ym, 0)
+
+        def own_core(self):
+            self.own("own_core", core)
             self.local.start()
 
-        def first_ring(self):
-            self.got(1, self.at(d, yb, l))
-            self.go(7, self.at(d, yb, l, 0), yp)
-            self.go(8, self.at(d, yb, l), core)
-            self.got(2, self.at(d, yn, l))
-            self.go(9, self.at(d, yn, l, 1), ym)
-            self.go(10, self.at(d, yn, l), core)
+        def own_x(self):
+            self.own("own_xl0", xl, 0)
+            self.own("own_xl1", xl, 1)
+
+        def forward(self):
+            self.got("own_yp0", d, yb, l, 0)
+            self.go("fwd_yp", yp, d, yb, l, 0)
+            self.got("own_ym1", d, yn, l, 1)
+            self.go("fwd_ym", ym, d, yn, l, 1)
+
+        def to_core(self):
+            self.got("own_yp1", d, yb, l, 1)
+            self.go("core_yb", core, d, yb, l)
+            self.got("own_ym0", d, yn, l, 0)
+            self.go("core_yn", core, d, yn, l)
 
         def pair(self):
-            ref = self.at(d, y, 1 - l)
-            self.got(0, ref)
-            self.go(4, ref, yp)
-            self.go(5, ref, ym)
-            self.go(6, ref, core)
-
-        def second_ring(self):
-            self.got(4, self.at(d, yb, 1 - l))
-            self.go(11, self.at(d, yb, 1 - l, 0), yp)
-            self.go(12, self.at(d, yb, 1 - l), core)
-            self.got(5, self.at(d, yn, 1 - l))
-            self.go(13, self.at(d, yn, 1 - l, 1), ym)
-            self.go(14, self.at(d, yn, 1 - l), core)
+            for p in range(2):
+                self.got(f"own_xl{p}", d, y, 1 - l, p)
+                self.go(f"pair_yp{p}", yp, d, y, 1 - l, p)
+                self.go(f"pair_ym{p}", ym, d, y, 1 - l, p)
+            self.go("core_pair", core, d, y, 1 - l)
+
+        def forward_pair(self):
+            self.got("pair_yp0", d, yb, 1 - l, 0)
+            self.go("last_yp", yp, d, yb, 1 - l, 0)
+            self.got("pair_ym1", d, yn, 1 - l, 1)
+            self.go("last_ym", ym, d, yn, 1 - l, 1)
+
+        def pair_to_core(self):
+            self.got("pair_yp1", d, yb, 1 - l, 1)
+            self.go("core_yb2", core, d, yb, 1 - l)
+            self.got("pair_ym0", d, yn, 1 - l, 0)
+            self.go("core_yn2", core, d, yn, 1 - l)
+
+        def far(self):
+            self.got("fwd_yp", d, yf, l, 0)
+            self.go("far0", core, d, yf, l, 0)
+            self.got("fwd_ym", d, yf, l, 1)
+            self.go("far1", core, d, yf, l, 1)
+
+        def far_pair(self):
+            self.got("last_yp", d, yf, 1 - l, 0)
+            self.go("far2", core, d, yf, 1 - l, 0)
+            self.got("last_ym", d, yf, 1 - l, 1)
+            self.go("far3", core, d, yf, 1 - l, 1)
 
         def near(self):
             self.local.wait()
-            self.got(3, self.at(1 - d, y, l))
-            self.got(6, self.at(1 - d, y, 1 - l))
-            self.got(8, self.at(1 - d, yb, l))
-            self.got(10, self.at(1 - d, yn, l))
-            self.got(12, self.at(1 - d, yb, 1 - l))
-            self.got(14, self.at(1 - d, yn, 1 - l))
-
-        def far(self):
-            self.got(7, self.at(d, yf, l, 0))
-            self.got(9, self.at(d, yf, l, 1))
-            self.go(15, self.at(d, yf, l), core)
-            self.got(11, self.at(d, yf, 1 - l, 0))
-            self.got(13, self.at(d, yf, 1 - l, 1))
-            self.go(16, self.at(d, yf, 1 - l), core)
+            self.got("own_core", 1 - d, y, l)
+            self.got("core_yb", 1 - d, yb, l)
+            self.got("core_yn", 1 - d, yn, l)
+            self.got("core_pair", 1 - d, y, 1 - l)
+            self.got("core_yb2", 1 - d, yb, 1 - l)
+            self.got("core_yn2", 1 - d, yn, 1 - l)
 
         def rest(self):
-            self.got(15, self.at(1 - d, yf, l))
-            self.got(16, self.at(1 - d, yf, 1 - l))
+            for p in range(2):
+                self.got(f"far{p}", 1 - d, yf, l, p)
+                self.got(f"far{2 + p}", 1 - d, yf, 1 - l, p)
 
     wqkv = Weight(wq, G, 384, ls.at[0])
     wout = Weight(wo, woG, 192, ls.at[1])
-    wqkv.own()
-
-    seg_id = net.ids(1)[0]
-    net.send(seg_id, segb.at[0], segb.at[1], core)
+
     st_ids = net.ids(7)
     for k in range(1, 8):
-        net.send(st_ids[k - 1], st.at[c], st.at[c], col_peers[k - 1])
+        net.send(st_ids[k - 1], st.at[c], st.at[c], col_peers[k - 1], lambda: st.at[0])
+    seg_id = net.ids(1)[0]
+    net.send(seg_id, segb.at[0], segb.at[1], core, lambda: segb.at[0])
+    wqkv.own_y()
+    pl.when(d == l)(wqkv.own_x)
+    wqkv.own_core()
     for k in range(1, 8):
         net.recv(st_ids[k - 1], st.at[(c + 8 - k) % 8], core)
     means = [st[k, 0:1, :] for k in range(8)]
@@ -184,20 +218,43 @@
     lanes = pl.ds(pl.multiple_of(c * 768, 768), 768)
     normed = (tok[...].astype(F32) - columns[:, 0:1]) * columns[:, 1:2]
     modulated = (normed * (1.0 + scale[0:1, lanes]) + shift[0:1, lanes]).astype(BF16)
+    mod[...] = modulated
     swap_ids = net.ids(2)
     halves = (pl.ds(0, 256), pl.ds(256, 256))
 
-    def keep_x():
-        Xg[c] = modulated
-
-    def swap_x():
-        mod[...] = modulated
-        for p in range(2):
-            net.send(swap_ids[p], mod.at[halves[p]], Xg.at[c, halves[p]], sw, keep=False)
-
-    both_sides(keep_x, swap_x)
-
-    net.recv(seg_id, segb.at[1], core)
+    xi = net.ids(14)
+
+    def xat(hh, zz, p):
+        return Xg.at[4 * hh + zz, halves[p]]
+
+    def xgo(i, ref, device, p, src=None):
+        net.send(xi[i], ref if src is None else src, ref, device, lambda: mod.at[halves[p]])
+
+    def xgot(i, ref):
+        net.recv(xi[i], ref, core)
+
+    def x_own(src):
+        for i, p, device in ((2, 0, zp), (5, 1, zm), (0, 0, xh), (3, 1, zp), (4, 0, zm), (1, 1, xh)):
+            xgo(i, xat(h, z, p), device, p, src(p))
+
+    def x_forward():
+        xgot(2, xat(h, zb, 0))
+        xgo(6, xat(h, zb, 0), zp, 0)
+        xgot(5, xat(h, zn, 1))
+        xgo(7, xat(h, zn, 1), zm, 1)
+
+    def x_pair(p):
+        i, a, b = ((0, 8, 10), (1, 9, 11))[p]
+        xgot(i, xat(h2, z, p))
+        xgo(a, xat(h2, z, p), zp, p)
+        xgo(b, xat(h2, z, p), zm, p)
+
+    def x_forward_pair():
+        xgot(8, xat(h2, zb, 0))
+        xgo(12, xat(h2, zb, 0), zp, 0)
+        xgot(11, xat(h2, zn, 1))
+        xgo(13, xat(h2, zn, 1), zm, 1)
+
     slot = jnp.where(d == l, 0, 1)
     lane_row = lax.broadcasted_iota(jnp.int32, (1, 128), 1).astype(F32)
 
@@ -221,50 +278,50 @@
             qx[j, rows, 128:256] = tile
         return carry
 
-    def wait_swap_x():
+    def start_kept():
+        x_own(lambda p: mod.at[halves[p]])
+        Xg[c] = mod[...]
+
+    def start_traded():
+        for p in range(2):
+            net.send(swap_ids[p], mod.at[halves[p]], Xg.at[c, halves[p]], sw, lambda p=p: mod.at[halves[p]], True)
+        wqkv.own_x()
+
+    both_sides(start_kept, start_traded)
+    net.recv(seg_id, segb.at[1], core)
+    lax.fori_loop(0, 32, fill, 0)
+    lax.fori_loop(0, 4, fill_q, 0)
+    wqkv.forward()
+
+    def kept():
+        x_forward()
+        wqkv.to_core()
+        x_pair(0)
+        wqkv.far()
+        x_pair(1)
+        wqkv.pair()
+        x_forward_pair()
+        wqkv.forward_pair()
+        wqkv.pair_to_core()
+
+    def traded():
+        wqkv.pair()
         for p in range(2):
             net.recv(swap_ids[p], Xg.at[c, halves[p]], sw)
-
-    pl.when(d != l)(wait_swap_x)
-
-    xi = net.ids(14)
-
-    def xat(hh, zz, p):
-        return Xg.at[4 * hh + zz, halves[p]]
-
-    def xgo(i, ref, device):
-        net.send(xi[i], ref, ref, device)
-
-    def xgot(i, ref):
-        net.recv(xi[i], ref, core)
-
-    xgo(2, xat(h, z, 0), zp)
-    xgo(5, xat(h, z, 1), zm)
-    xgo(0, xat(h, z, 0), xh)
-    xgo(1, xat(h, z, 1), xh)
-    xgo(3, xat(h, z, 1), zp)
-    xgo(4, xat(h, z, 0), zm)
-
-    lax.fori_loop(0, 32, fill, 0)
-    lax.fori_loop(0, 4, fill_q, 0)
-
-    wqkv.first_ring()
-    xgot(2, xat(h, zb, 0))
-    xgo(6, xat(h, zb, 0), zp)
-    xgot(5, xat(h, zn, 1))
-    xgo(7, xat(h, zn, 1), zm)
-    wqkv.pair()
-    xgot(0, xat(h2, z, 0))
-    xgo(8, xat(h2, z, 0), zp)
-    xgo(10, xat(h2, z, 0), zm)
-    xgot(1, xat(h2, z, 1))
-    xgo(11, xat(h2, z, 1), zm)
-    xgo(9, xat(h2, z, 1), zp)
-    wqkv.second_ring()
-    xgot(8, xat(h2, zb, 0))
-    xgo(12, xat(h2, zb, 0), zp)
-    xgot(11, xat(h2, zn, 1))
-    xgo(13, xat(h2, zn, 1), zm)
+        x_own(lambda p: None)
+        wqkv.to_core()
+        x_forward()
+        wqkv.far()
+        wqkv.forward_pair()
+        wqkv.pair_to_core()
+        x_pair(0)
+        x_pair(1)
+        x_forward_pair()
+
+    both_sides(kept, traded)
+    wout.own_y()
+    wout.own_x()
+    wout.own_core()
 
     a0 = yf
     delta = (zf + 4 - yf) % 4
@@ -291,8 +348,7 @@
         return carry
 
     lax.fori_loop(0, 4, early, 0)
-    wqkv.far()
-    wout.own()
+    wqkv.far_pair()
     xgot(6, xat(h, zf, 0))
     xgot(7, xat(h, zf, 1))
     xgot(12, xat(h2, zf, 0))
@@ -309,9 +365,11 @@
             return carry
 
         lax.fori_loop(0, 4, late, 0)
-        qx[j, :, 0:128] = (rms(acc[j, :, 0:128]) * gain[j]).astype(BF16)
         kvx[j, rr, :, 256:384] = rms(acc[j, :, 128:256]).astype(BF16)
         kvx[j, rr, :, 128:256] = acc[j, :, 256:384].astype(BF16)
+
+    def finish_query(j):
+        qx[j, :, 0:128] = (rms(acc[j, :, 0:128]) * gain[j]).astype(BF16)
 
     ki = [net.ids(8) for _ in range(3)]
 
@@ -319,8 +377,9 @@
         rows = pl.ds(0, 512) if p is None else halves[p]
         return kvx.at[j, 2 * yy + dd, rows, pl.ds(128, 256)]
 
-    def kgo(j, i, ref, device):
-        net.send(ki[j][i], ref, ref, device)
+    def kgo(j, i, ref, device, p=None):
+        like = lambda: kvx.at[0, 0, pl.ds(0, 512) if p is None else halves[p], pl.ds(128, 256)]
+        net.send(ki[j][i], ref, ref, device, like)
 
     def kgot(j, i, ref):
         net.recv(ki[j][i], ref, core)
@@ -333,10 +392,10 @@
 
     def kv_forward(j):
         kgot(j, 0, kat(j, yb, d))
-        kgo(j, 3, kat(j, yb, d, 0), yp)
+        kgo(j, 3, kat(j, yb, d, 0), yp, 0)
         kgo(j, 4, kat(j, yb, d), core)
         kgot(j, 1, kat(j, yn, d))
-        kgo(j, 5, kat(j, yn, d, 1), ym)
+        kgo(j, 5, kat(j, yn, d, 1), ym, 1)
         kgo(j, 6, kat(j, yn, d), core)
 
     def kv_far(j):
@@ -388,8 +447,9 @@
         ref = attg.at[j, 4 * hh + zz]
         return ref if p is None else ref.at[halves[p]]
 
-    def ago(j, i, ref, device):
-        net.send(ai[j][i], ref, ref, device)
+    def ago(j, i, ref, device, p=None):
+        like = lambda: ast.at[0] if p is None else ast.at[0, halves[p]]
+        net.send(ai[j][i], ref, ref, device, like)
 
     def agot(j, i, ref):
         net.recv(ai[j][i], ref, core)
@@ -402,7 +462,7 @@
 
         def swap():
             ast[j] = value
-            net.send(ai[j][9], ast.at[j], attg.at[j, c], sw, keep=False)
+            net.send(ai[j][9], ast.at[j], attg.at[j, c], sw, lambda: ast.at[0], True)
 
         both_sides(keep, swap)
 
@@ -415,18 +475,18 @@
 
     def att_forward(j):
         agot(j, 1, aat(j, h, zb))
-        ago(j, 3, aat(j, h, zb, 0), zp)
+        ago(j, 3, aat(j, h, zb, 0), zp, 0)
         agot(j, 2, aat(j, h, zn))
-        ago(j, 4, aat(j, h, zn, 1), zm)
+        ago(j, 4, aat(j, h, zn, 1), zm, 1)
         agot(j, 0, aat(j, h2, z))
         ago(j, 5, aat(j, h2, z), zp)
         ago(j, 6, aat(j, h2, z), zm)
 
     def att_second(j):
         agot(j, 5, aat(j, h2, zb))
-        ago(j, 7, aat(j, h2, zb, 0), zp)
+        ago(j, 7, aat(j, h2, zb, 0), zp, 0)
         agot(j, 6, aat(j, h2, zn))
-        ago(j, 8, aat(j, h2, zn, 1), zm)
+        ago(j, 8, aat(j, h2, zn, 1), zm, 1)
 
     def att_rest(j):
         agot(j, 3, aat(j, h, zf, 0))
@@ -453,71 +513,78 @@
     finish(0)
     kv_own(0)
     finish(1)
+    kv_own(1)
     finish(2)
+    for j in range(3):
+        finish_query(j)
     attend_here(0)
     kv_forward(0)
-    kv_own(1)
+    kv_own(2)
     attend_near(0)
     kv_far(0)
+    kv_forward(1)
     attend_far(0)
     att_put(0)
-    kv_forward(1)
-    kv_own(2)
+    attend_here(1)
     att_own(0)
-    attend_here(1)
     attend_near(1)
+    kv_forward(2)
+    wout.pair()
+    wout.forward()
+    kv_far(1)
     att_forward(0)
-    kv_far(1)
     attend_far(1)
     att_put(1)
-    kv_forward(2)
+    attend_here(2)
     att_own(1)
-    att_second(0)
-    wout.pair()
-    wout.first_ring()
-    attend_here(2)
     attend_near(2)
     kv_far(2)
-    att_forward(1)
+    att_second(0)
     attend_far(2)
     att_put(2)
+    att_forward(1)
+    wout.to_core()
+    wout.far()
     att_own(2)
-    wout.second_ring()
+    wout.forward_pair()
+    wout.pair_to_core()
+    bacc[...] = jnp.zeros_like(bacc)
     att_second(1)
-    bacc[...] = jnp.zeros_like(bacc)
+    att_rest(0)
     att_forward(2)
-    wout.far()
-    att_rest(0)
+    wout.far_pair()
+    att_second(2)
     wout.near()
     wout.rest()
     project_out(0)
-    att_second(2)
     att_rest(1)
     project_out(1)
     att_rest(2)
     project_out(2)
     out[...] = (gate[...] * bacc[...]).astype(BF16)
 
-    for copy in net.sent:
-        copy.wait_send()
+    for i, (like, some) in net.sent.items():
+        if not some:
+            net.copy(i, like(), like(), core).wait_send()
 
     @pl.when(d != l)
     def _():
-        for p in range(2):
-            net.copy(swap_ids[p], mod.at[halves[p]], Xg.at[c, halves[p]], sw).wait_send()
-        for j in range(3):
-            net.copy(ai[j][9], ast.at[j], attg.at[j, c], sw).wait_send()
+        for i, (like, some) in net.sent.items():
+            if some:
+                net.copy(i, like(), like(), core).wait_send()
 
 
 def local(tokens, w_qkv, w_out, ada_shift, ada_scale, out_gate, head_gain, block_segment):
     vmem = pl.BlockSpec(memory_space=pltpu.VMEM)
     smem = pl.BlockSpec(memory_space=pltpu.SMEM)
+    anyw = pl.BlockSpec(memory_space=pl.ANY)
     return pl.pallas_call(
         kernel,
         out_shape=jax.ShapeDtypeStruct((512, 768), BF16),
-        in_specs=[vmem] * 6 + [smem] * 2,
+        in_specs=[anyw] * 3 + [vmem] * 3 + [smem] * 2,
         out_specs=vmem,
         scratch_shapes=[
+            pltpu.VMEM((512, 768), BF16),
             pltpu.VMEM((16, 384, 1152), BF16),
             pltpu.VMEM((8, 512, 768), BF16),
             pltpu.VMEM((3, 8, 512, 512), BF16),
@@ -533,7 +600,7 @@
             pltpu.VMEM((2, 32, 128), F32),
             pltpu.SemaphoreType.DMA((N_FLOWS,)),
             pltpu.SemaphoreType.DMA((N_FLOWS,)),
-            pltpu.SemaphoreType.DMA((2,)),
+            pltpu.SemaphoreType.DMA((3,)),
         ],
         compiler_params=pltpu.CompilerParams(
             collective_id=0, has_side_effects=True, vmem_limit_bytes=60 * 2**20

time: 156 us -> 146 us (0.936)
  Pallas kernels: 152 us -> 143 us
    pallas_call x1, Pallas kernels: 152 us -> 143 us  [local(): pl.pallas_call(kernel, out_shape=jax.ShapeDtypeStruct((512, 768), BF16),...]
where the time goes in v3:
time: 146 us; the launch traced here: 145 us
  Pallas kernels  143 us (98%)
  local copies, waits for them, and re-layouts  2.06 us (1%)
    pallas_call x1, Pallas kernels, local(): pl.pallas_call(kernel, out_shape=jax.ShapeDtypeStruct((512, 768), BF16),...  143 us

profile of v3, /device:TPU:1, one launch (start us, length us, event | category | flops | bytes accessed | tf_op | source)
XLA Modules:
  0.0 145.1 jit_solution(5683286835311265872)
XLA Ops:
  0.0 143.0 %shard_map.82 = bf16[512,768]{1,0:T(8,128)(2,1)} custom-call(bf16[512,768]{1,0:T(8,128)(2,1)} %tok_hbm.1, bf16[384,1152]{1,0:T(8,128)(2,1)} %wq.1, bf16[192,768]{1,0:T(8,128)(2,1)} %wo.1, f32[1,6144]{1,0:T(1,128)} %shift.1, f32[1,6144]{1,0:T(1,128)} %scale.1, f32[1,768]{1,0:T(1,128)} %gate.1, f32[3]{0:T(128)} %gain.1, s32[1,32]{1,0:T(1,128)} %seg.1), custom_call_target="tpu_custom_call" | custom-call | tf_op jit(solution)/shard_map/pallas_call | solution.py:581
  143.0 2.1 %copy.10 = bf16[512,768]{1,0:T(8,128)(2,1)} copy(bf16[512,768]{1,0:T(8,128)(2,1)} %shard_map.82) | data formatting | bytes 1572864

commit v4 on v3

--- a/solution.py
+++ b/solution.py
@@ -10,7 +10,7 @@
 HD = 128
 BLK = 128
 EPS = 1e-06
-FAR = 2048.0
+FAR = 256.0
 F32 = jnp.float32
 BF16 = jnp.bfloat16
 MESH = pl.DeviceIdType.MESH
@@ -343,8 +343,7 @@
 
     def early(s, carry):
         block = 4 * (s % 2) + jnp.where(s < 2, e0, e1)
-        for j in range(3):
-            acc[j] += product(block, j)
+        acc[0] += product(block, 0)
         return carry
 
     lax.fori_loop(0, 4, early, 0)
@@ -355,6 +354,8 @@
     xgot(13, xat(h2, zf, 1))
     wqkv.rest()
 
+    power = (1.0 / HD**0.5) * math.log2(math.e)
+
     def rms(v):
         return v * lax.rsqrt(jnp.mean(v * v, axis=-1, keepdims=True) + EPS)
 
@@ -364,12 +365,19 @@
             acc[j] += product(block, j)
             return carry
 
-        lax.fori_loop(0, 4, late, 0)
+        def whole(block, carry):
+            acc[j] += product(block, j)
+            return carry
+
+        if j == 0:
+            lax.fori_loop(0, 4, late, 0)
+        else:
+            lax.fori_loop(0, 8, whole, 0)
         kvx[j, rr, :, 256:384] = rms(acc[j, :, 128:256]).astype(BF16)
         kvx[j, rr, :, 128:256] = acc[j, :, 256:384].astype(BF16)
 
     def finish_query(j):
-        qx[j, :, 0:128] = (rms(acc[j, :, 0:128]) * gain[j]).astype(BF16)
+        qx[j, :, 0:128] = (rms(acc[j, :, 0:128]) * (gain[j] * power)).astype(BF16)
 
     ki = [net.ids(8) for _ in range(3)]
 
@@ -398,17 +406,10 @@
         kgo(j, 5, kat(j, yn, d, 1), ym, 1)
         kgo(j, 6, kat(j, yn, d), core)
 
-    def kv_far(j):
-        kgot(j, 3, kat(j, yf, d, 0))
-        kgot(j, 5, kat(j, yf, d, 1))
-        kgo(j, 7, kat(j, yf, d), core)
-
-    power = (1.0 / HD**0.5) * math.log2(math.e)
-
     def attend(j, amount, row_of):
         def step(s, carry):
-            key_row = row_of(s // 2)
-            rows = pl.ds(pl.multiple_of((s % 2) * 256, 256), 256)
+            key_row = row_of(s)
+            rows = pl.ds(0, 512)
 
             @pl.when(jnp.abs(key_row - rr) <= 4)
             def _():
@@ -418,14 +419,20 @@
                     (((1,), (1,)), ((), ())),
                     preferred_element_type=F32,
                 )
-                weights = jnp.exp2(scores * power).astype(BF16)
+                weights = jnp.exp2(scores).astype(BF16)
                 oacc[rows, :] += jnp.dot(
                     weights, kvx[j, key_row, :, 0:256], preferred_element_type=F32
                 )
 
             return carry
 
-        lax.fori_loop(0, 2 * amount, step, 0)
+        lax.fori_loop(0, amount, step, 0)
+
+    def kv_far(j):
+        kgot(j, 3, kat(j, yf, d, 0))
+        kgot(j, 5, kat(j, yf, d, 1))
+        kgo(j, 7, kat(j, yf, d), core)
+        attend(j, 1, lambda k: 2 * yf + d)
 
     def attend_here(j):
         oacc[...] = jnp.zeros_like(oacc)
@@ -439,7 +446,7 @@
 
     def attend_far(j):
         kgot(j, 7, kat(j, yf, 1 - d))
-        attend(j, 2, lambda k: 2 * yf + k)
+        attend(j, 1, lambda k: 2 * yf + 1 - d)
 
     ai = [net.ids(10) for _ in range(3)]
 

time: 146 us -> 141 us (0.966)
  Pallas kernels: 143 us -> 139 us
    pallas_call x1, Pallas kernels: 143 us -> 139 us  [local(): pl.pallas_call(kernel, out_shape=jax.ShapeDtypeStruct((512, 768), BF16),...]
where the time goes in v4:
time: 141 us
  Pallas kernels  139 us (99%)
  local copies, waits for them, and re-layouts  2.06 us (1%)
    pallas_call x1, Pallas kernels, local(): pl.pallas_call(kernel, out_shape=jax.ShapeDtypeStruct((512, 768), BF16),...  139 us

profile of v4, /device:TPU:1, one launch (start us, length us, event | category | flops | bytes accessed | tf_op | source)
XLA Modules:
  0.0 140.7 jit_solution(17076822306063227633)
XLA Ops:
  0.0 138.6 %shard_map.82 = bf16[512,768]{1,0:T(8,128)(2,1)} custom-call(bf16[512,768]{1,0:T(8,128)(2,1)} %tok_hbm.1, bf16[384,1152]{1,0:T(8,128)(2,1)} %wq.1, bf16[192,768]{1,0:T(8,128)(2,1)} %wo.1, f32[1,6144]{1,0:T(1,128)} %shift.1, f32[1,6144]{1,0:T(1,128)} %scale.1, f32[1,768]{1,0:T(1,128)} %gate.1, f32[3]{0:T(128)} %gain.1, s32[1,32]{1,0:T(1,128)} %seg.1), custom_call_target="tpu_custom_call" | custom-call | tf_op jit(solution)/shard_map/pallas_call | solution.py:588
  138.6 2.1 %copy.10 = bf16[512,768]{1,0:T(8,128)(2,1)} copy(bf16[512,768]{1,0:T(8,128)(2,1)} %shard_map.82) | data formatting | bytes 1572864

commit v5 on v4

--- a/solution.py
+++ b/solution.py
@@ -10,11 +10,11 @@
 HD = 128
 BLK = 128
 EPS = 1e-06
-FAR = 256.0
+FAR = 2048.0
 F32 = jnp.float32
 BF16 = jnp.bfloat16
 MESH = pl.DeviceIdType.MESH
-N_FLOWS = 128
+N_FLOWS = 160
 
 
 class Net:
@@ -72,8 +72,8 @@
     tok_copy.start()
 
     barrier = pltpu.get_barrier_semaphore()
-    col_peers = [(d, row, (c + k) % 8) for k in range(1, 8)]
-    for peer in col_peers + [core, xl, yp, ym]:
+    z_peers = [(d, row, 4 * h + (z + k) % 4) for k in range(1, 4)]
+    for peer in z_peers + [xh, core, xl, yp, ym]:
         pl.semaphore_signal(barrier, inc=1, device_id=peer, device_id_type=MESH)
 
     @pl.when(d != l)
@@ -90,8 +90,8 @@
     part_sq = jnp.sum(off * off, axis=-1, keepdims=True)
     lane = lax.broadcasted_iota(jnp.int32, (512, 128), 1)
     columns = jnp.where(lane == 0, part_mean, jnp.where(lane == 1, part_sq, 0.0))
-    st[c] = columns.T[:8]
-    pl.semaphore_wait(barrier, 11 + (d + l) % 2)
+    st[z, h] = columns.T[:8]
+    pl.semaphore_wait(barrier, 8 + (d + l) % 2)
 
     def wid(dd, yy, ll):
         return 8 * dd + 2 * yy + ll
@@ -198,19 +198,21 @@
     wqkv = Weight(wq, G, 384, ls.at[0])
     wout = Weight(wo, woG, 192, ls.at[1])
 
-    st_ids = net.ids(7)
-    for k in range(1, 8):
-        net.send(st_ids[k - 1], st.at[c], st.at[c], col_peers[k - 1], lambda: st.at[0])
+    st_ids = net.ids(4)
+    net.send(st_ids[0], st.at[z, h], st.at[z, h], xh, lambda: st.at[0, 0])
     seg_id = net.ids(1)[0]
     net.send(seg_id, segb.at[0], segb.at[1], core, lambda: segb.at[0])
     wqkv.own_y()
     pl.when(d == l)(wqkv.own_x)
     wqkv.own_core()
-    for k in range(1, 8):
-        net.recv(st_ids[k - 1], st.at[(c + 8 - k) % 8], core)
-    means = [st[k, 0:1, :] for k in range(8)]
+    net.recv(st_ids[0], st.at[z, h2], xh)
+    for k in range(1, 4):
+        net.send(st_ids[k], st.at[z], st.at[z], z_peers[k - 1], lambda: st.at[0])
+    for k in range(1, 4):
+        net.recv(st_ids[k], st.at[(z + 4 - k) % 4], core)
+    means = [st[k // 2, k % 2, 0:1, :] for k in range(8)]
     mean = sum(means) * 0.125
-    total_sq = sum(st[k, 1:2, :] for k in range(8))
+    total_sq = sum(st[k // 2, k % 2, 1:2, :] for k in range(8))
     total_sq = total_sq + 768.0 * sum((m - mean) * (m - mean) for m in means)
     inv = lax.rsqrt(total_sq * (1.0 / 6144.0) + EPS)
     sub = lax.broadcasted_iota(jnp.int32, (128, 512), 0)
@@ -377,7 +379,7 @@
         kvx[j, rr, :, 128:256] = acc[j, :, 256:384].astype(BF16)
 
     def finish_query(j):
-        qx[j, :, 0:128] = (rms(acc[j, :, 0:128]) * (gain[j] * power)).astype(BF16)
+        qx[j, :, 0:128] = (rms(acc[j, :, 0:128]) * gain[j]).astype(BF16)
 
     ki = [net.ids(8) for _ in range(3)]
 
@@ -419,7 +421,7 @@
                     (((1,), (1,)), ((), ())),
                     preferred_element_type=F32,
                 )
-                weights = jnp.exp2(scores).astype(BF16)
+                weights = jnp.exp2(scores * power).astype(BF16)
                 oacc[rows, :] += jnp.dot(
                     weights, kvx[j, key_row, :, 0:256], preferred_element_type=F32
                 )
@@ -448,58 +450,70 @@
         kgot(j, 7, kat(j, yf, 1 - d))
         attend(j, 1, lambda k: 2 * yf + 1 - d)
 
-    ai = [net.ids(10) for _ in range(3)]
-
-    def aat(j, hh, zz, p=None):
-        ref = attg.at[j, 4 * hh + zz]
-        return ref if p is None else ref.at[halves[p]]
-
-    def ago(j, i, ref, device, p=None):
-        like = lambda: ast.at[0] if p is None else ast.at[0, halves[p]]
-        net.send(ai[j][i], ref, ref, device, like)
-
-    def agot(j, i, ref):
-        net.recv(ai[j][i], ref, core)
+    ai = [net.ids(16) for _ in range(3)]
+
+    def aat(j, hh, zz, p):
+        return attg.at[j, 4 * hh + zz, halves[p]]
+
+    def ago(j, i, hh, zz, p, device):
+        net.send(ai[j][i], aat(j, hh, zz, p), aat(j, hh, zz, p), device, lambda: ast.at[0, halves[p]])
+
+    def agot(j, i, hh, zz, p):
+        net.recv(ai[j][i], aat(j, hh, zz, p), core)
+
+    def att_send(j, p):
+        for i, device in (((2, zp), (0, xh), (4, zm)), ((5, zm), (1, xh), (3, zp)))[p]:
+            ago(j, i, h, z, p, device)
 
     def att_put(j):
-        value = (oacc[:, 128:256] / oacc[:, 0:128]).astype(BF16)
-
-        def keep():
-            attg[j, c] = value
-
-        def swap():
-            ast[j] = value
-            net.send(ai[j][9], ast.at[j], attg.at[j, c], sw, lambda: ast.at[0], True)
-
-        both_sides(keep, swap)
+        def keep(p, value):
+            attg[j, c, halves[p], :] = value
+            att_send(j, p)
+
+        def swap(p, value):
+            ast[j, halves[p], :] = value
+            like = lambda: ast.at[0, halves[p]]
+            net.send(ai[j][14 + p], ast.at[j, halves[p]], attg.at[j, c, halves[p]], sw, like, True)
+
+        for p in range(2):
+            value = (oacc[halves[p], 128:256] / oacc[halves[p], 0:128]).astype(BF16)
+            pl.when(d == l)(lambda: keep(p, value))
+            pl.when(d != l)(lambda: swap(p, value))
 
     def att_own(j):
-        pl.when(d != l)(lambda: net.recv(ai[j][9], attg.at[j, c], sw))
-        me = aat(j, h, z)
-        ago(j, 0, me, xh)
-        ago(j, 1, me, zp)
-        ago(j, 2, me, zm)
+        def traded_own():
+            for p in range(2):
+                agot(j, 14 + p, h, z, p)
+                att_send(j, p)
+
+        pl.when(d != l)(traded_own)
 
     def att_forward(j):
-        agot(j, 1, aat(j, h, zb))
-        ago(j, 3, aat(j, h, zb, 0), zp, 0)
-        agot(j, 2, aat(j, h, zn))
-        ago(j, 4, aat(j, h, zn, 1), zm, 1)
-        agot(j, 0, aat(j, h2, z))
-        ago(j, 5, aat(j, h2, z), zp)
-        ago(j, 6, aat(j, h2, z), zm)
+        agot(j, 2, h, zb, 0)
+        ago(j, 6, h, zb, 0, zp)
+        agot(j, 5, h, zn, 1)
+        ago(j, 7, h, zn, 1, zm)
+        agot(j, 0, h2, z, 0)
+        ago(j, 8, h2, z, 0, zp)
+        ago(j, 10, h2, z, 0, zm)
+        agot(j, 1, h2, z, 1)
+        ago(j, 11, h2, z, 1, zm)
+        ago(j, 9, h2, z, 1, zp)
 
     def att_second(j):
-        agot(j, 5, aat(j, h2, zb))
-        ago(j, 7, aat(j, h2, zb, 0), zp, 0)
-        agot(j, 6, aat(j, h2, zn))
-        ago(j, 8, aat(j, h2, zn, 1), zm, 1)
+        agot(j, 8, h2, zb, 0)
+        ago(j, 12, h2, zb, 0, zp)
+        agot(j, 11, h2, zn, 1)
+        ago(j, 13, h2, zn, 1, zm)
 
     def att_rest(j):
-        agot(j, 3, aat(j, h, zf, 0))
-        agot(j, 4, aat(j, h, zf, 1))
-        agot(j, 7, aat(j, h2, zf, 0))
-        agot(j, 8, aat(j, h2, zf, 1))
+        agot(j, 3, h, zb, 1)
+        agot(j, 4, h, zn, 0)
+        agot(j, 9, h2, zb, 1)
+        agot(j, 10, h2, zn, 0)
+        for p in range(2):
+            agot(j, 6 + p, h, zf, p)
+            agot(j, 12 + p, h2, zf, p)
 
     def wrows(block, j):
         pieces = []
@@ -549,10 +563,10 @@
     att_second(0)
     attend_far(2)
     att_put(2)
+    wout.to_core()
     att_forward(1)
-    wout.to_core()
+    att_own(2)
     wout.far()
-    att_own(2)
     wout.forward_pair()
     wout.pair_to_core()
     bacc[...] = jnp.zeros_like(bacc)
@@ -603,7 +617,7 @@
             pltpu.VMEM((512, 768), F32),
             pltpu.VMEM((512, 768), BF16),
             pltpu.VMEM((3, 512, 128), BF16),
-            pltpu.VMEM((8, 8, 512), F32),
+            pltpu.VMEM((4, 2, 8, 512), F32),
             pltpu.VMEM((2, 32, 128), F32),
             pltpu.SemaphoreType.DMA((N_FLOWS,)),
             pltpu.SemaphoreType.DMA((N_FLOWS,)),

time: 141 us -> 139 us (0.986)
  Pallas kernels: 139 us -> 137 us
    pallas_call x1, Pallas kernels: 139 us -> 137 us  [local(): pl.pallas_call(kernel, out_shape=jax.ShapeDtypeStruct((512, 768), BF16),...]
where the time goes in v5:
time: 139 us
  Pallas kernels  137 us (99%)
  local copies, waits for them, and re-layouts  2.06 us (1%)
    pallas_call x1, Pallas kernels, local(): pl.pallas_call(kernel, out_shape=jax.ShapeDtypeStruct((512, 768), BF16),...  137 us

profile of v5, /device:TPU:1, one launch (start us, length us, event | category | flops | bytes accessed | tf_op | source)
XLA Modules:
  0.0 139.0 jit_solution(15196780153354806648)
XLA Ops:
  0.0 136.9 %shard_map.82 = bf16[512,768]{1,0:T(8,128)(2,1)} custom-call(bf16[512,768]{1,0:T(8,128)(2,1)} %tok_hbm.1, bf16[384,1152]{1,0:T(8,128)(2,1)} %wq.1, bf16[192,768]{1,0:T(8,128)(2,1)} %wo.1, f32[1,6144]{1,0:T(1,128)} %shift.1, f32[1,6144]{1,0:T(1,128)} %scale.1, f32[1,768]{1,0:T(1,128)} %gate.1, f32[3]{0:T(128)} %gain.1, s32[1,32]{1,0:T(1,128)} %seg.1), custom_call_target="tpu_custom_call" | custom-call | tf_op jit(solution)/shard_map/pallas_call | solution.py:602
  136.9 2.1 %copy.10 = bf16[512,768]{1,0:T(8,128)(2,1)} copy(bf16[512,768]{1,0:T(8,128)(2,1)} %shard_map.82) | data formatting | bytes 1572864

commit v6 on v5

--- a/solution.py
+++ b/solution.py
@@ -332,9 +332,9 @@
     e1 = (a0 + jnp.where(third == 3, 2, 3)) % 4
     e2 = (a0 + third) % 4
 
-    def product(block, j):
+    def product(block, first, last):
         left = Xg[block]
-        cols = slice(384 * j, 384 * (j + 1))
+        cols = slice(first, last)
         right = jnp.concatenate([G[2 * block, :, cols], G[2 * block + 1, :, cols]], axis=0)
         return jnp.dot(left, right, preferred_element_type=F32)
 
@@ -345,7 +345,7 @@
 
     def early(s, carry):
         block = 4 * (s % 2) + jnp.where(s < 2, e0, e1)
-        acc[0] += product(block, 0)
+        acc[:, 0:384] += product(block, 0, 384)
         return carry
 
     lax.fori_loop(0, 4, early, 0)
@@ -354,6 +354,12 @@
     xgot(7, xat(h, zf, 1))
     xgot(12, xat(h2, zf, 0))
     xgot(13, xat(h2, zf, 1))
+
+    def third_blocks(s, carry):
+        acc[:, 0:384] += product(4 * s + e2, 0, 384)
+        return carry
+
+    lax.fori_loop(0, 2, third_blocks, 0)
     wqkv.rest()
 
     power = (1.0 / HD**0.5) * math.log2(math.e)
@@ -361,25 +367,25 @@
     def rms(v):
         return v * lax.rsqrt(jnp.mean(v * v, axis=-1, keepdims=True) + EPS)
 
+    def add_last(first, last):
+        def step(s, carry):
+            acc[:, first:last] += product(4 * s + a0, first, last)
+            return carry
+
+        lax.fori_loop(0, 2, step, 0)
+
+    def add_heads(block, carry):
+        acc[:, 384:1152] += product(block, 384, 1152)
+        return carry
+
     def finish(j):
-        def late(s, carry):
-            block = 4 * (s % 2) + jnp.where(s < 2, e2, a0)
-            acc[j] += product(block, j)
-            return carry
-
-        def whole(block, carry):
-            acc[j] += product(block, j)
-            return carry
-
-        if j == 0:
-            lax.fori_loop(0, 4, late, 0)
-        else:
-            lax.fori_loop(0, 8, whole, 0)
-        kvx[j, rr, :, 256:384] = rms(acc[j, :, 128:256]).astype(BF16)
-        kvx[j, rr, :, 128:256] = acc[j, :, 256:384].astype(BF16)
+        base = 384 * j
+        kvx[j, rr, :, 256:384] = rms(acc[:, base + 128 : base + 256]).astype(BF16)
+        kvx[j, rr, :, 128:256] = acc[:, base + 256 : base + 384].astype(BF16)
 
     def finish_query(j):
-        qx[j, :, 0:128] = (rms(acc[j, :, 0:128]) * gain[j]).astype(BF16)
+        base = 384 * j
+        qx[j, :, 0:128] = (rms(acc[:, base : base + 128]) * gain[j]).astype(BF16)
 
     ki = [net.ids(8) for _ in range(3)]
 
@@ -531,10 +537,13 @@
 
         lax.fori_loop(0, 4, step, 0)
 
+    add_last(128, 384)
     finish(0)
     kv_own(0)
+    lax.fori_loop(0, 8, add_heads, 0)
     finish(1)
     kv_own(1)
+    add_last(0, 128)
     finish(2)
     for j in range(3):
         finish_query(j)
@@ -547,9 +556,9 @@
     attend_far(0)
     att_put(0)
     attend_here(1)
-    att_own(0)
     attend_near(1)
     kv_forward(2)
+    att_own(0)
     wout.pair()
     wout.forward()
     kv_far(1)
@@ -557,12 +566,12 @@
     attend_far(1)
     att_put(1)
     attend_here(2)
-    att_own(1)
     attend_near(2)
     kv_far(2)
-    att_second(0)
+    att_own(1)
     attend_far(2)
     att_put(2)
+    att_second(0)
     wout.to_core()
     att_forward(1)
     att_own(2)
@@ -612,7 +621,7 @@
             pltpu.VMEM((3, 512, 256), BF16),
             pltpu.VMEM((16, 192, 768), BF16),
             pltpu.VMEM((3, 8, 512, 128), BF16),
-            pltpu.VMEM((3, 512, 384), F32),
+            pltpu.VMEM((512, 1152), F32),
             pltpu.VMEM((512, 256), F32),
             pltpu.VMEM((512, 768), F32),
             pltpu.VMEM((512, 768), BF16),

time: 139 us -> 138 us (level)
  no operation moved by 1% of the time
where the time goes in v6:
time: 138 us
  Pallas kernels  136 us (99%)
  local copies, waits for them, and re-layouts  2.06 us (1%)
    pallas_call x1, Pallas kernels, local(): pl.pallas_call(kernel, out_shape=jax.ShapeDtypeStruct((512, 768), BF16),...  136 us

profile of v6, /device:TPU:1, one launch (start us, length us, event | category | flops | bytes accessed | tf_op | source)
XLA Modules:
  0.0 138.0 jit_solution(10040845245535440573)
XLA Ops:
  0.0 135.9 %shard_map.82 = bf16[512,768]{1,0:T(8,128)(2,1)} custom-call(bf16[512,768]{1,0:T(8,128)(2,1)} %tok_hbm.1, bf16[384,1152]{1,0:T(8,128)(2,1)} %wq.1, bf16[192,768]{1,0:T(8,128)(2,1)} %wo.1, f32[1,6144]{1,0:T(1,128)} %shift.1, f32[1,6144]{1,0:T(1,128)} %scale.1, f32[1,768]{1,0:T(1,128)} %gate.1, f32[3]{0:T(128)} %gain.1, s32[1,32]{1,0:T(1,128)} %seg.1), custom_call_target="tpu_custom_call" | custom-call | tf_op jit(solution)/shard_map/pallas_call | solution.py:611
  135.9 2.1 %copy.10 = bf16[512,768]{1,0:T(8,128)(2,1)} copy(bf16[512,768]{1,0:T(8,128)(2,1)} %shard_map.82) | data formatting | bytes 1572864

commit v7 on v6

--- a/solution.py
+++ b/solution.py
@@ -448,9 +448,10 @@
         attend(j, 2, lambda k: 2 * y + k)
 
     def attend_near(j):
+        attend(j, 2, lambda k: 2 * ((y + 3 + 2 * k) % 4) + d)
         kgot(j, 4, kat(j, yb, 1 - d))
         kgot(j, 6, kat(j, yn, 1 - d))
-        attend(j, 4, lambda k: 2 * ((y + 3 + 2 * (k // 2)) % 4) + k % 2)
+        attend(j, 2, lambda k: 2 * ((y + 3 + 2 * k) % 4) + 1 - d)
 
     def attend_far(j):
         kgot(j, 7, kat(j, yf, 1 - d))

time: 138 us -> 138 us (level)
  no operation moved by 1% of the time
where the time goes in v7:
time: 138 us
  Pallas kernels  136 us (99%)
  local copies, waits for them, and re-layouts  2.06 us (1%)
    pallas_call x1, Pallas kernels, local(): pl.pallas_call(kernel, out_shape=jax.ShapeDtypeStruct((512, 768), BF16),...  136 us

profile of v7, /device:TPU:1, one launch (start us, length us, event | category | flops | bytes accessed | tf_op | source)
XLA Modules:
  0.0 138.0 jit_solution(4966690245222026977)
XLA Ops:
  0.0 135.9 %shard_map.82 = bf16[512,768]{1,0:T(8,128)(2,1)} custom-call(bf16[512,768]{1,0:T(8,128)(2,1)} %tok_hbm.1, bf16[384,1152]{1,0:T(8,128)(2,1)} %wq.1, bf16[192,768]{1,0:T(8,128)(2,1)} %wo.1, f32[1,6144]{1,0:T(1,128)} %shift.1, f32[1,6144]{1,0:T(1,128)} %scale.1, f32[1,768]{1,0:T(1,128)} %gate.1, f32[3]{0:T(128)} %gain.1, s32[1,32]{1,0:T(1,128)} %seg.1), custom_call_target="tpu_custom_call" | custom-call | tf_op jit(solution)/shard_map/pallas_call | solution.py:612
  135.9 2.1 %copy.10 = bf16[512,768]{1,0:T(8,128)(2,1)} copy(bf16[512,768]{1,0:T(8,128)(2,1)} %shard_map.82) | data formatting | bytes 1572864
